TPU v7x, 32 devices: a whole 2x2x4 slice. The times are simulated.
32 devices in a mesh: seq: 8 (over z, x), batch: 4 (over y, core).
Axes of the slice: x: 2, y: 2, z: 4, core: 2. Of those that a mesh axis runs over, the one named last changes fastest.
Arguments:
- tokens: bfloat16 [8, 2048, 512], P('batch', 'seq'), may hold values from -7 to 7
- doc_lengths: int32 [8, 16], P('batch'), may hold values from 1 to 1792, as said below
- cotangent: bfloat16 [8, 2048, 512], P('batch', 'seq'), may hold values from -6 to 6
- mixer_weights: float32 [4096, 512], P(('seq', 'batch'))
- mlp_weights: float32 [4096, 512], P(('seq', 'batch'))
- small_params: float32 [3072], P(('seq', 'batch')), may hold values from -16 to 5
- mixer_first: float32 [4096, 512], P(('seq', 'batch'))
- mixer_second: float32 [4096, 512], P(('seq', 'batch'))
- mlp_first: float32 [4096, 512], P(('seq', 'batch'))
- mlp_second: float32 [4096, 512], P(('seq', 'batch'))
- small_first: float32 [3072], P(('seq', 'batch'))
- small_second: float32 [3072], P(('seq', 'batch'))
Outputs:
- output: bfloat16 [8, 2048, 512], P('batch', 'seq')
- input_grad: bfloat16 [8, 2048, 512], P('batch', 'seq')
- mixer_grad: float32 [4096, 512], P(('seq', 'batch'))
- mlp_grad: float32 [4096, 512], P(('seq', 'batch'))
- small_grad: float32 [3072], P(('seq', 'batch'))
- mixer_first_new: float32 [4096, 512], P(('seq', 'batch'))
- mixer_second_new: float32 [4096, 512], P(('seq', 'batch'))
- mlp_first_new: float32 [4096, 512], P(('seq', 'batch'))
- mlp_second_new: float32 [4096, 512], P(('seq', 'batch'))
- small_first_new: float32 [3072], P(('seq', 'batch'))
- small_second_new: float32 [3072], P(('seq', 'batch'))
- mixer_new: float32 [4096, 512], P(('seq', 'batch'))
- mlp_new: float32 [4096, 512], P(('seq', 'batch'))
- small_new: float32 [3072], P(('seq', 'batch'))
- mixer_copy: bfloat16 [4096, 512], P(('seq', 'batch'))
- mlp_copy: bfloat16 [4096, 512], P(('seq', 'batch'))
- small_copy: bfloat16 [3072], P(('seq', 'batch'))
- tensor_norms: float32 [2, 10], replicated
- trust_ratios: float32 [10], replicated
Inputs may be any that keep to these rules, and one draw needn't show every extreme that they name: `doc_lengths`: each stream's lengths sum to between 2016 and 2047. In every group of 2 consecutive streams one stream holds a document of exactly 1792 positions, its second, starting within the first 64 positions.
All inputs are finite; a program needn't handle non-finite values.
Results may differ from a plain program's by a relative error of at most 0.012.
Values may be sent and summed in bfloat16 or wider, within the bound.
No kernel may reach another device: no remote copies, remote signals or barrier semaphores. Data moves between devices by JAX's collectives and lax.ppermute only.
A program may use at most 128 MiB of HBM per device.

v0:
```python
import functools

import jax
import jax.numpy as jnp
from jax import lax
from jax.experimental import pallas as pl
from jax.experimental.pallas import tpu as pltpu
from jax.sharding import PartitionSpec as P

D = 512
H = 1024
FF = 2048
STEP = 5
SEG = 8
ROWS = 128
PLANES = 4
HALF = PLANES * ROWS
GATES = 3
ROLES = 4
TAIL = 16
SMALL_BLOCKS = 3
Z, X, Y, CORE, SEQ, DEVICE, MIXER_ROLE, MLP_ROLE = range(8)

first_decay = 0.5
second_decay = 0.5
learn_rate = 0.25
matrix_decay = 0.01
moment_eps = 1e-06

f32 = jnp.float32
bf16 = jnp.bfloat16
AXES = ("seq", "batch")

PLANE_BITS = ((0, 0), (0, 2), (1, 0), (1, 2))


def dot_nt(a, b):
    return lax.dot_general(a, b, (((1,), (1,)), ((), ())), preferred_element_type=f32)


def dot_nn(a, b):
    return lax.dot_general(a, b, (((1,), (0,)), ((), ())), preferred_element_type=f32)


def dot_tn(a, b):
    return lax.dot_general(a, b, (((0,), (0,)), ((), ())), preferred_element_type=f32)


def exchange(value, seq_bits, batch_bits, targets=None):
    seqs, batches = lax.axis_size("seq"), lax.axis_size("batch")
    pairs = [
        (s * batches + b, (s ^ seq_bits) * batches + (b ^ batch_bits))
        for s in range(seqs)
        for b in range(batches)
        if targets is None or (s ^ seq_bits) in targets
    ]
    return lax.ppermute(value, AXES, pairs)


def unit(x):
    return lax.rsqrt(jnp.mean(x * x, axis=-1, keepdims=True) + 1e-05)


def rms_back(x, d_normed, gain):
    scale = unit(x)
    normal = x * scale
    d_unit = d_normed * gain
    mean = jnp.mean(d_unit * normal, axis=-1, keepdims=True)
    return jnp.sum(d_normed * normal, axis=0, keepdims=True), scale * (d_unit - normal * mean)


def gather_roles(slabs, held):
    for role in range(GATES):
        for q, ref in enumerate(slabs):
            held[role, pl.ds(q * ROWS, ROWS)] = ref[pl.ds(role * ROWS, ROWS), :]


def group(s, steps, j):
    return pl.ds(pl.multiple_of((s * steps + j) * SEG, SEG), SEG)


def pair(s, steps, j):
    return pl.ds(pl.multiple_of((s * steps + 2 * j) * SEG, 2 * SEG), 2 * SEG)


def segment_order(block):
    row = lax.broadcasted_iota(jnp.int32, (block, block), 0)
    position = lax.broadcasted_iota(jnp.int32, (block, block), 1)
    return jnp.where(position == (row % SEG) * (block // SEG) + row // SEG, 1.0, 0.0).astype(bf16)


def inward(ref):
    order = segment_order(ref.shape[1])
    return jnp.concatenate([dot_nn(order, ref[s]) for s in range(2)], axis=0)


def outward(ref, value):
    block = ref.shape[1]
    order = segment_order(block)
    for s in range(2):
        ref[s] = dot_tn(order, value[s * block : (s + 1) * block]).astype(bf16)


def z_of(ids_ref, k, core):
    return ids_ref[Z] ^ (jnp.where(core == 0, k, 3 - k) if k in (1, 2) else k)


def pack_kernel(ids_ref, weights_ref, got_ref, small_ref, out_ref, held, sem):
    copy = pltpu.make_async_copy(small_ref, held, sem)
    copy.start()
    out_ref[pl.ds(0, ROWS), :] = weights_ref[...]
    copy.wait()
    mine, other = held[...], got_ref[...]
    rest = jnp.zeros((1, ROWS - mine.shape[1]), f32)
    core = ids_ref[CORE]
    lines = [jnp.where(core == 0, mine, other), rest, jnp.where(core == 0, other, mine), rest]
    line = jnp.concatenate(lines + [jnp.zeros((1, D - 2 * ROWS), f32)], axis=1)
    out_ref[pl.ds(ROWS, TAIL), :] = jnp.broadcast_to(line, (TAIL, D)).astype(bf16)


def slab_kernel(ids_ref, early_ref, late_ref, *refs):
    slab_ref, lines = refs[-2:]
    lines[...] = jnp.zeros_like(lines)
    for k in range(ROLES):
        part = (early_ref, late_ref)[k // 2].at[k % 2]
        role = z_of(ids_ref, k, ids_ref[CORE])
        slab_ref[pl.ds(pl.multiple_of(role * ROWS, ROWS), ROWS), :] = part[pl.ds(0, ROWS), :]
        lines[pl.ds(role, 1), :] = part[pl.ds(ROWS, TAIL), :].astype(f32)[0:1]
    slab_ref[pl.ds(ROLES * ROWS, TAIL), :] = lines[...].astype(bf16)


def marks_kernel(ids_ref, lengths_ref, restart_ref, valid_ref):
    block = restart_ref.shape[0] // 2
    row = lax.broadcasted_iota(jnp.int32, (block, 1), 0)
    position = ids_ref[SEQ] * block + (row % SEG) * (block // SEG) + row // SEG
    for s in range(2):
        begins = jnp.zeros((block, 1), jnp.bool_)
        end = 0
        for k in range(lengths_ref.shape[1]):
            begins = begins | (position == end)
            end = end + lengths_ref[s, k]
        begins = begins | (position == end)
        restart_ref[pl.ds(s * block, block), :] = jnp.where(begins, 0.0, 1.0)
        valid_ref[pl.ds(s * block, block), :] = jnp.where(position < end, 1.0, 0.0)


def stack_kernel(first_ref, second_ref, *refs):
    out_ref = refs[-1]
    if first_ref.shape == out_ref.shape[1:]:
        out_ref[0], out_ref[1] = first_ref[...], second_ref[...]
    else:
        count = first_ref.shape[0]
        out_ref[:count], out_ref[count:] = first_ref[...], second_ref[...]


def normed_kernel(tok_ref, gain_ref, normed_ref):
    normed_ref[...] = first_norm(tok_ref, gain_ref)


def relay_kernel(bit, forward, flipped, ids_ref, group_ref, other_ref, *refs):
    late = ((ids_ref[SEQ] & bit) != 0) == forward
    mine, other = group_ref[...], other_ref[...]
    if flipped:
        quarter = HALF // 2
        at = (quarter, 0, 3 * quarter, 2 * quarter)
        other = jnp.concatenate([other[:, k : k + quarter] for k in at], axis=1)
    if bit == 1:
        decay, state = jnp.ones_like(mine[:2]), jnp.zeros_like(mine[:2])
    else:
        decay, state = refs[0][0:2, :], refs[0][2:4, :]
    state = jnp.where(late, decay * other[2:] + state, state)
    if refs[-1].shape[0] == 2:
        refs[-1][...] = state
        return
    group_out, before_out = refs[-2:]
    before_out[...] = jnp.concatenate([jnp.where(late, decay * other[:2], decay), state], axis=0)
    first, second = jnp.where(late, other, mine), jnp.where(late, mine, other)
    group_out[...] = jnp.concatenate([first[:2] * second[:2], second[:2] * first[2:] + second[2:]], axis=0)


def relay_far_kernel(forward, ids_ref, before_ref, *refs):
    terms, state_ref = refs[:ROLES], refs[-1]
    z = ids_ref[Z]
    state = jnp.zeros_like(state_ref)
    for place in range(ROLES - 1):
        source = place if forward else ROLES - 1 - place
        term = terms[0][...]
        for k in range(1, ROLES):
            term = jnp.where((z ^ source) == k, terms[k][...], term)
        earlier = (source < z) if forward else (source > z)
        state = jnp.where(earlier, term[2:] + term[:2] * state, state)
    state_ref[...] = before_ref[2:4, :] + before_ref[0:2, :] * state


def gate_shares(f, i):
    most = jnp.maximum(jnp.maximum(-f, -i), 0.0)
    one, low_f, low_i = jnp.exp(-most), jnp.exp(-f - most), jnp.exp(-i - most)
    inverse = 1.0 / ((one + low_i) + (one + low_f))
    return (one + low_i) * inverse, (one + low_f) * inverse, low_f * inverse, low_i * inverse


def first_norm(tok_ref, gain_ref):
    x = inward(tok_ref)
    return (x * unit(x) * gain_ref[...]).astype(bf16)


def unpack(count, ids_ref, slabs, by_device, flat):
    chips = [2 * (ids_ref[X] ^ (k // 2)) + (ids_ref[Y] ^ (k % 2)) for k in range(PLANES)]
    for k, ref in enumerate(slabs):
        lines = ref[pl.ds(ROLES * ROWS, TAIL), :].astype(f32)
        for z in range(ROLES):
            for core in range(2):
                row = z * 2 * PLANES + 2 * chips[k] + core
                by_device[pl.ds(row, 1), :] = lines[z : z + 1, core * ROWS : (core + 1) * ROWS]
    parts = [by_device[pl.ds(k, 8, stride=4), :] for k in range(4)]
    for k in range(3):
        cut = ROWS - (k + 1) * (ROWS - count)
        row = jnp.concatenate([parts[k][:, k * (ROWS - count) : count], parts[k + 1][:, : ROWS - cut]], axis=1)
        flat[pl.ds(k, 8, stride=3), :] = row
    rows = [flat[pl.ds(k, 1), :] for k in range(2 * PLANES)]
    yield jnp.concatenate(rows[:PLANES], axis=1)
    yield jnp.concatenate(rows[PLANES:], axis=1)
    for base in (2 * PLANES, 4 * PLANES):
        for half in range(2):
            at = [base + 2 * chips[k] + (ids_ref[CORE] ^ half) for k in range(PLANES)]
            yield jnp.concatenate([flat[pl.ds(row, 1), :] for row in at], axis=1)


def scan_halves(normed, f_bias, i_bias, rs_ref, held, both_ref, tot_ref, columns, sega_ref, segb_ref, f_ref, i_ref, c_ref):
    for role, ref in enumerate((f_ref, i_ref, c_ref)):
        ref[...] = dot_nt(normed, held[role])
    steps = normed.shape[0] // (2 * SEG)

    def step(j, carry):
        after = []
        for s in range(2):
            at = group(s, steps, j)
            keep, share, _, _ = gate_shares(f_ref[at, :] + f_bias, i_ref[at, :] + i_bias)
            a = keep * rs_ref[at, :]
            b = a * carry[s][1] + share * c_ref[at, :]
            both_ref[0, at, :] = a
            both_ref[1, at, :] = b
            after.append((a * carry[s][0], b))
        return tuple(after)

    start = (jnp.ones((SEG, HALF), f32), jnp.zeros((SEG, HALF), f32))
    ends = lax.fori_loop(0, steps, step, (start, start), unroll=steps)
    for s, (seg_a, seg_b) in enumerate(ends):
        sega_ref[pl.ds(s * SEG, SEG), :] = seg_a
        segb_ref[pl.ds(s * SEG, SEG), :] = seg_b
        tot_a, tot_b = seg_a[0:1], seg_b[0:1]
        for k in range(1, SEG):
            a = seg_a[k : k + 1]
            tot_a, tot_b = a * tot_a, a * tot_b + seg_b[k : k + 1]
        tot_ref[pl.ds(s, 1), columns] = tot_a
        tot_ref[pl.ds(2 + s, 1), columns] = tot_b


def scan_first_kernel(count, ids_ref, tok_ref, rs_ref, *refs):
    slabs, outs, scratch = refs[:PLANES], refs[PLANES:-5], refs[-5:]
    normed_ref, gain_one_ref, gain_two_ref, fo_ref, fp_ref, io_ref, ip_ref, held, both_ref, tot_ref, sega_ref, segb_ref = outs
    f_ref, i_ref, c_ref, by_device, flat = scratch
    gather_roles(slabs, held)
    small = unpack(count, ids_ref, slabs, by_device, flat)
    for ref, value in zip((gain_one_ref, gain_two_ref, fo_ref, fp_ref, io_ref, ip_ref), small, strict=True):
        ref[...] = value
    normed_ref[...] = first_norm(tok_ref, gain_one_ref)
    scan_halves(
        normed_ref[...], fo_ref[...], io_ref[...], rs_ref, held, both_ref, tot_ref, pl.ds(0, HALF),
        sega_ref, segb_ref, f_ref, i_ref, c_ref,
    )


def scan_kernel(first, normed_ref, rs_ref, fb_ref, ib_ref, *refs):
    if not first:
        earlier_ref, *refs = refs
    slabs, (held, both_ref, tot_ref, sega_ref, segb_ref, f_ref, i_ref, c_ref) = refs[:PLANES], refs[-8:]
    gather_roles(slabs, held)
    if not first:
        tot_ref[:, pl.ds(0, HALF)] = earlier_ref[...]
    scan_halves(
        normed_ref[...], fb_ref[...], ib_ref[...], rs_ref, held, both_ref, tot_ref,
        pl.ds(0 if first else HALF, HALF), sega_ref, segb_ref, f_ref, i_ref, c_ref,
    )


def dout_kernel(cot_ref, valid_ref, *refs):
    refs[-1][...] = (inward(cot_ref) * valid_ref[...]).astype(bf16)


def terms_kernel(normed_ref, fb_ref, ib_ref, held, *refs):
    share_ref, df_ref, di_ref, cand_ref, f_ref, i_ref = refs[-6:]
    normed = normed_ref[...]
    for role, ref in enumerate((f_ref, i_ref, cand_ref)):
        ref[...] = dot_nt(normed, held[role])
    f_bias, i_bias = fb_ref[...], ib_ref[...]

    def step(j, carry):
        at = pl.ds(pl.multiple_of(j * 2 * SEG, 2 * SEG), 2 * SEG)
        keep, share, slow_f, slow_i = gate_shares(f_ref[at, :] + f_bias, i_ref[at, :] + i_bias)
        share_ref[at, :] = share
        df_ref[at, :] = keep * slow_f
        di_ref[at, :] = share * slow_i
        return carry

    lax.fori_loop(0, normed.shape[0] // (2 * SEG), step, 0, unroll=8)


def states_kernel(inc_ref, tok_ref, gain_ref, both_o, both_p, sega_o, sega_p, segb_o, segb_p, *refs):
    slabs, refs = refs[: 2 * PLANES], refs[2 * PLANES :]
    states_o, states_p, low_o, low_p, resid_ref, normed_ref, held = refs
    steps = resid_ref.shape[0] // (2 * SEG)
    halves = (
        (both_o, sega_o, segb_o, states_o, low_o, 0),
        (both_p, sega_p, segb_p, states_p, low_p, HALF),
    )
    start = []
    for _, sega, segb, _, _, column in halves:
        for s in range(2):
            seg_a, seg_b = sega[pl.ds(s * SEG, SEG), :], segb[pl.ds(s * SEG, SEG), :]
            at_seg = [inc_ref[pl.ds(s, 1), pl.ds(column, HALF)]]
            for k in range(SEG - 1):
                at_seg.append(seg_a[k : k + 1] * at_seg[-1] + seg_b[k : k + 1])
            start.append(jnp.concatenate(at_seg, axis=0))

    def step(j, carry):
        after = []
        for k, (both, _, _, states, low, _) in enumerate(halves):
            for s in range(2):
                carried, two = carry[2 * k + s], []
                for q in range(2):
                    at = group(s, steps, 2 * j + q)
                    carried = both[0, at, :] * carried
                    two.append(both[1, at, :] + carried)
                    states[at, :] = two[-1]
                low[pair(s, steps, j), :] = jnp.concatenate(two, axis=0).astype(bf16)
                after.append(carried)
        return tuple(after)

    lax.fori_loop(0, steps // 2, step, tuple(start), unroll=steps // 2)
    r = inward(tok_ref)
    for q, ref in enumerate(slabs):
        held[0, pl.ds(q * ROWS, ROWS)] = ref[pl.ds(GATES * ROWS, ROWS), :]
    for low, k in zip((low_o, low_p), range(2), strict=True):
        r = r + dot_nn(low[...], held[0, pl.ds(k * HALF, HALF)])
    resid_ref[...] = r
    normed_ref[...] = (r * unit(r) * gain_ref[...]).astype(bf16)


GELU_A = 0.7978845608028654
GELU_B = 0.044715


def mlp_kernel(ids_ref, normed_ref, resid_ref, dout_ref, gain_ref, *refs):
    parts, refs = refs[:4], refs[4:]
    dresid_ref, dgain_ref, gown_ref, gnear_ref, gfar_ref, act_ref, held, dnorm_ref = refs

    def bring(at):
        for half in range(2):
            for k in range(ROLES):
                role = z_of(ids_ref, k, ids_ref[CORE] ^ half)
                held[at, half, pl.ds(role, 1)] = parts[2 * half + k // 2][k % 2, at].reshape(1, ROWS, D)

    bring(0)
    dnorm_ref[...] = jnp.zeros_like(dnorm_ref)

    normed, dout = normed_ref[...], dout_ref[...]

    def ahead(i):
        at, low = i // 2, i % 2
        if low == 1 and at + 1 < PLANES:
            bring(at + 1)
        w_up = held[at, :, low].reshape(2 * ROWS, D)
        w_down = held[at, :, low + 2].reshape(2 * ROWS, D)
        return dot_nt(normed, w_up), dot_nt(dout, w_down), w_up, w_down

    now = ahead(0)
    for i in range(2 * PLANES):
        inner, d_act, w_up, w_down = now
        if i + 1 < 2 * PLANES:
            now = ahead(i + 1)
        square = inner * inner
        curve = jnp.tanh(inner * (GELU_A + GELU_A * GELU_B * square))
        half = 0.5 + 0.5 * curve
        activated = (inner * half).astype(bf16)
        slope = half + (half - half * half) * (inner * (2.0 * GELU_A + 6.0 * GELU_A * GELU_B * square))
        d_inner = (slope * d_act).astype(bf16)
        act_ref[i] = activated
        dnorm_ref[...] += dot_nn(d_inner, w_up)
        g_up = dot_tn(d_inner, normed).astype(bf16).reshape(2, ROWS, D)
        g_down = dot_tn(activated, dout).astype(bf16).reshape(2, ROWS, D)
        q = i // 2
        for k, ref in enumerate((gown_ref.at[q], (gnear_ref, gfar_ref)[q // 2].at[q % 2])):
            ref[i % 2] = g_up[k]
            ref[i % 2 + 2] = g_down[k]
    r = resid_ref[...]
    dgain_ref[...], d_r = rms_back(r, dnorm_ref[...], gain_ref[...])
    dresid_ref[...] = dout_ref[...].astype(f32) + d_r


def back_kernel(dresid_ref, low_o, low_p, retain_o, retain_p, sega_o, sega_p, held, *refs):
    acc_o, acc_p, tot_ref, segb_o, segb_p, gown_ref, gpar_ref = refs
    steps = dresid_ref.shape[0] // (2 * SEG)
    dmix = dresid_ref[...].astype(bf16)
    for acc, k in zip((acc_o, acc_p), range(2), strict=True):
        acc[...] = dot_nt(dmix, held[0, pl.ds(k * HALF, HALF)])
    halves = ((retain_o, acc_o), (retain_p, acc_p))

    def step(n, carry):
        after = []
        for k, (retain, acc) in enumerate(halves):
            for s in range(2):
                at = group(s, steps, steps - 1 - n)
                back = acc[at, :] + carry[2 * k + s]
                acc[at, :] = back
                after.append(retain[0, at, :] * back)
        return tuple(after)

    ends = lax.fori_loop(0, steps, step, (jnp.zeros((SEG, HALF), f32),) * 4, unroll=steps)
    for k, (sega, segb) in enumerate(((sega_o, segb_o), (sega_p, segb_p))):
        for s in range(2):
            emitted = ends[2 * k + s]
            segb[pl.ds(s * SEG, SEG), :] = emitted
            seg_a = sega[pl.ds(s * SEG, SEG), :]
            tot_a, tot_b = seg_a[SEG - 1 :], emitted[SEG - 1 :]
            for q in reversed(range(SEG - 1)):
                a = seg_a[q : q + 1]
                tot_a, tot_b = a * tot_a, a * tot_b + emitted[q : q + 1]
            tot_ref[pl.ds(s, 1), pl.ds(k * HALF, HALF)] = tot_a
            tot_ref[pl.ds(2 + s, 1), pl.ds(k * HALF, HALF)] = tot_b
    for low, ref in ((low_o, gown_ref), (low_p, gpar_ref)):
        ref[...] = dot_tn(low[...], dmix).astype(bf16).reshape(PLANES, 1, ROWS, D)


def gates_kernel(
    column, arr_ref, inc_ref, acc_ref, sega_ref, segb_ref, share_ref, df_ref, di_ref, cand_ref, retain_ref, states_ref,
    rs_ref, normed_ref, order_ref, grad_ref, pf_ref, pi_ref, pc_ref, dfb_ref, dib_ref,
):
    steps = normed_ref.shape[0] // (2 * SEG)
    start, first = [], []
    for s in range(2):
        seg_a, seg_b = sega_ref[pl.ds(s * SEG, SEG), :], segb_ref[pl.ds(s * SEG, SEG), :]
        at_seg = [arr_ref[pl.ds(s, 1), pl.ds(column, HALF)]]
        for k in reversed(range(1, SEG)):
            at_seg.append(seg_a[k : k + 1] * at_seg[-1] + seg_b[k : k + 1])
        start.append(jnp.concatenate(at_seg[::-1], axis=0))
        ends = states_ref[group(s, steps, steps - 1), :]
        first.append(jnp.concatenate([inc_ref[pl.ds(s, 1), pl.ds(column, HALF)], ends[: SEG - 1]], axis=0))

    def step(n, carry):
        *carried, sum_f, sum_i = carry
        m = steps // 2 - 1 - n
        for s in range(2):
            terms = []
            for q in (1, 0):
                j = 2 * m + q
                at = group(s, steps, j)
                back = acc_ref[at, :] + carried[s]
                carried[s] = carried[s] * retain_ref[0, at, :]
                previous = states_ref[group(s, steps, jnp.maximum(j - 1, 0)), :]
                if q == 0:
                    previous = jnp.where(m == 0, first[s], previous)
                both_ways = back * (previous * rs_ref[at, :] - cand_ref[at, :])
                d_f = both_ways * df_ref[at, :]
                d_i = both_ways * di_ref[at, :]
                sum_f = sum_f + d_f
                sum_i = sum_i - d_i
                terms.append((d_f, -d_i, back * share_ref[at, :]))
            for late, early, ref in zip(*terms, (pf_ref, pi_ref, pc_ref), strict=True):
                ref[pair(s, steps, m), :] = jnp.concatenate([early, late], axis=0).astype(bf16)
        return (*carried, sum_f, sum_i)

    nothing = jnp.zeros((SEG, HALF), f32)
    *_, sum_f, sum_i = lax.fori_loop(0, steps // 2, step, (*start, nothing, nothing), unroll=steps // 2)
    dfb_ref[...] = jnp.sum(sum_f, axis=0, keepdims=True)
    dib_ref[...] = jnp.sum(sum_i, axis=0, keepdims=True)
    normed = normed_ref[...]
    for role, ref in enumerate((pf_ref, pi_ref, pc_ref)):
        grad_ref[:, role] = dot_tn(ref[...], normed).astype(bf16).reshape(PLANES, ROWS, D)


def input_terms_kernel(ids_ref, tok_ref, dgain_two_ref, dfb_o, dfb_p, dib_o, dib_p, *refs):
    terms, weights, refs = refs[: 2 * GATES], refs[2 * GATES : 2 * GATES + 2], refs[-3:]
    dnorm_ref, small_ref, rows_ref = refs
    d_normed = 0.0
    for role in range(GATES):
        for k in range(2):
            d_normed = d_normed + dot_nn(terms[k * GATES + role][...], weights[k][role])
    dnorm_ref[...] = d_normed
    x = inward(tok_ref)
    d_gain = jnp.sum(d_normed * (x * unit(x)), axis=0, keepdims=True)
    for k in range(PLANES):
        rows_ref[pl.ds(k, 1), :] = d_gain[:, k * ROWS : (k + 1) * ROWS]
        rows_ref[pl.ds(PLANES + k, 1), :] = dgain_two_ref[:, pl.ds(k * ROWS, ROWS)]
        chip = 4 * (ids_ref[X] ^ (k // 2)) + 2 * (ids_ref[Y] ^ (k % 2))
        for core, (fb, ib) in enumerate(((dfb_o, dib_o), (dfb_p, dib_p))):
            row = 2 * PLANES + chip + (ids_ref[CORE] ^ core)
            rows_ref[pl.ds(row, 1), :] = fb[:, pl.ds(k * ROWS, ROWS)]
            rows_ref[pl.ds(row + 2 * PLANES, 1), :] = ib[:, pl.ds(k * ROWS, ROWS)]
    blocks = [rows_ref[pl.ds(k * SEG, SEG), :] for k in range(SMALL_BLOCKS)] + [jnp.zeros((SEG, ROWS), f32)]
    small_ref[...] = jnp.concatenate([jnp.concatenate(blocks, axis=1), jnp.zeros((SEG, D), f32)], axis=0)


def outputs_kernel(tok_ref, gain_ref, dresid_ref, dnorm_ref, resid_ref, valid_ref, act_ref, held, order_ref, dx_ref, output_ref, done_ref):
    done_ref[...] = jnp.zeros_like(done_ref)
    _, d_x = rms_back(inward(tok_ref), dnorm_ref[...], gain_ref[...])
    outward(dx_ref, (dresid_ref[...] + d_x).astype(bf16))
    total = resid_ref[...]
    for i in range(2 * PLANES):
        total = total + dot_nn(act_ref[i], held[i // 2, :, i % 2 + 2].reshape(2 * ROWS, D))
    outward(output_ref, (total * valid_ref[...]).astype(bf16))


def out_place(core, k):
    return jnp.where(core == 0, 3 - k, k) if k in (1, 2) else k


def mlp_pair_kernel(ids_ref, own_ref, got_ref, out_ref, outgot_ref, *refs):
    for q in range(2):
        ref = refs[-1].at[q]
        ref[pl.ds(0, ROLES)] = (own_ref[2 + q].astype(f32) + got_ref[q].astype(f32)).astype(bf16)
        at = pl.ds(out_place(ids_ref[CORE], 2 + q), 1)
        ref[pl.ds(ROLES, 1)] = (out_ref[at, 0].astype(f32) + outgot_ref[at, 0].astype(f32)).astype(bf16)


def gate_pair_kernel(own_ref, got_ref, small_ref, small_got, *outs):
    small = (small_ref[...] + small_got[...]).astype(bf16)
    for k, ref in enumerate(outs[-PLANES:]):
        total = (own_ref[k].astype(f32) + got_ref[k].astype(f32)).astype(bf16)
        ref[pl.ds(0, GATES * ROWS), :] = total.reshape(GATES * ROWS, D)
        ref[pl.ds(GATES * ROWS, TAIL), :] = small


def half_sum_kernel(ids_ref, own_ref, pair_ref, out_ref, outpair_ref, got_ref, *refs):
    keep_ref, send_ref, out_keep, out_send = refs[-4:]
    z = ids_ref[Z]
    near_bit = jnp.where(ids_ref[CORE] == 0, 1, 2)
    for q in range(2):

        def total(role, q=q):
            at = pl.ds(role, 1)
            terms = own_ref[q, at].astype(f32) + pair_ref[q, at].astype(f32)
            return (terms + got_ref[q, at].astype(f32)).astype(bf16).reshape(ROWS, D)

        for k, role in enumerate((z, z ^ near_bit ^ 3)):
            keep_ref[k, q] = total(role)
            send_ref[k, q] = total(role ^ near_bit)
        at = pl.ds(out_place(ids_ref[CORE], q), 1)
        terms = out_ref[at, 0].astype(f32) + outpair_ref[at, 0].astype(f32)
        (out_keep, out_send)[q][...] = (terms + got_ref[q, pl.ds(ROLES, 1)].astype(f32)).astype(bf16).reshape(ROWS, D)


def mlp_far_kernel(keep_ref, got_ref, *refs):
    stay_ref, send_ref = refs[-2:]
    stay_ref[...] = (keep_ref[0].astype(f32) + got_ref[0].astype(f32)).astype(bf16)
    send_ref[...] = (keep_ref[1].astype(f32) + got_ref[1].astype(f32)).astype(bf16)


def mlp_last_kernel(stay_ref, got_ref, *refs):
    keep_ref, send_ref = refs[-2:]
    keep_ref[...] = stay_ref[0].astype(f32) + got_ref[0].astype(f32)
    send_ref[...] = (stay_ref[1].astype(f32) + got_ref[1].astype(f32)).astype(bf16)


def gate_plane_kernel(ids_ref, p0, p1, p2, p3, out_ref, out_got, *refs):
    z = ids_ref[Z]
    keep_ref, s1_ref, s2_ref, s3_ref = refs[-4:]

    def total(at):
        terms = [ref[at, :].astype(f32) for ref in (p0, p1, p2, p3)]
        return (terms[0] + terms[1]) + (terms[2] + terms[3])

    def of_role(role):
        at = pl.ds(pl.multiple_of(jnp.minimum(role, GATES - 1) * ROWS, ROWS), ROWS)
        return jnp.where(role == GATES, out_ref[...].astype(f32) + out_got[...].astype(f32), total(at))

    small = total(pl.ds(GATES * ROWS, TAIL))
    keep_ref[pl.ds(0, ROWS), :] = of_role(z)
    keep_ref[pl.ds(ROWS, TAIL), :] = small
    for k, ref in enumerate((s1_ref, s2_ref, s3_ref)):
        ref[pl.ds(0, ROWS), :] = of_role(z ^ (k + 1)).astype(bf16)
        ref[pl.ds(ROWS, TAIL), :] = small.astype(bf16)


def joined(at, keep_ref, gots):
    total = keep_ref[at, :]
    for ref in gots:
        total = total + ref[at, :].astype(f32)
    return total


def matrix_step(at, keep_ref, gots, weight_ref, first_ref, second_ref, outs):
    grad_ref, first_out, second_out, dir_ref = outs
    weight = weight_ref[...]
    gradient = joined(at, keep_ref, gots)
    grad_ref[...] = gradient
    first_out[...], second_out[...], direction = moments(
        weight, gradient, first_ref[...], second_ref[...], matrix_decay
    )
    dir_ref[...] = direction
    return weight, direction


def square_rows(value):
    square = jnp.sum((value * value).reshape(-1, SEG, D), axis=0)
    return (square[:, :128] + square[:, 128:256]) + (square[:, 256:384] + square[:, 384:])


def moments_kernel(keep_ref, got_ref, weight_ref, first_ref, second_ref, *outs):
    *outs, wsum_ref, dsum_ref = outs
    weight, direction = matrix_step(
        pl.ds(0, weight_ref.shape[0]), keep_ref, [got_ref], weight_ref, first_ref, second_ref, outs
    )
    wsum_ref[...] = square_rows(weight)
    dsum_ref[...] = square_rows(direction)


def finish_kernel(
    ids_ref, keep_ref, g1_ref, g2_ref, g3_ref, wsum_f, dsum_f,
    mixer_ref, mixer_first, mixer_second, weight_ref, first_ref, second_ref,
    mixer_grad, mixer_first_out, mixer_second_out, mixer_dir, grad_ref, first_out, second_out, dir_ref, squares_ref,
    rows_ref,
):
    gots = (g1_ref, g2_ref, g3_ref)
    mixer_rows = mixer_ref.shape[0]
    mixer_values = matrix_step(
        pl.ds(0, mixer_rows), keep_ref, gots, mixer_ref, mixer_first, mixer_second,
        (mixer_grad, mixer_first_out, mixer_second_out, mixer_dir),
    )
    total = joined(pl.ds(mixer_rows, TAIL), keep_ref, gots)
    rows_ref[...] = jnp.zeros_like(rows_ref)
    for k in range(SMALL_BLOCKS):
        rows_ref[pl.ds(k * SEG, SEG), :] = total[:SEG, k * ROWS : (k + 1) * ROWS]
    weight = weight_ref[...]
    count = weight.shape[1]
    start = ids_ref[DEVICE] * count
    row, lane = start // ROWS, start % ROWS
    two = jnp.concatenate([rows_ref[pl.ds(row, 1), :], rows_ref[pl.ds(row + 1, 1), :]], axis=1)
    two = jnp.broadcast_to(two, (SEG, 2 * ROWS))
    gradient = pltpu.roll(two, (2 * ROWS - lane) % (2 * ROWS), 1)[:1, :count]
    grad_ref[...] = gradient
    first_out[...], second_out[...], direction = moments(weight, gradient, first_ref[...], second_ref[...], 0.0)
    dir_ref[...] = direction
    place = start + lax.broadcasted_iota(jnp.int32, (1, count), 1)
    at = lax.broadcasted_iota(jnp.int32, (1, ROWS), 1)
    bounds = (0, D, 2 * D, 2 * D + H, 2 * D + 2 * H)
    lines = []
    for mixer_value, mlp_sum, value in zip(mixer_values, (wsum_f, dsum_f), (weight, direction), strict=True):
        line = jnp.where(at == ids_ref[MIXER_ROLE], jnp.sum(square_rows(mixer_value), keepdims=True), 0.0)
        line = line + jnp.where(at == ROLES + ids_ref[MLP_ROLE], jnp.sum(mlp_sum[...], keepdims=True), 0.0)
        for k in range(4):
            inside = (place >= bounds[k]) & (place < bounds[k + 1])
            part = jnp.sum(jnp.where(inside, value * value, 0.0), axis=1, keepdims=True)
            line = line + jnp.where(at == ROLES + 2 + k, part, 0.0)
        lines.append(line)
    squares_ref[...] = jnp.concatenate(lines + [jnp.zeros((SEG - 2, ROWS), f32)], axis=0)


def ratio_of(squares_ref, tensor):
    norms = jnp.sqrt(squares_ref[0:2, :])
    ratios = norms[0:1] / (norms[1:2] + 1e-06)
    at = lax.broadcasted_iota(jnp.int32, (1, ROWS), 1)
    return jnp.sum(jnp.where(at == tensor, ratios, 0.0), axis=1, keepdims=True)


def new_weights(ratio, weight_ref, dir_ref, new_ref, copy_ref):
    value = weight_ref[...] - learn_rate * ratio * dir_ref[...]
    new_ref[...] = value
    copy_ref[...] = value.astype(bf16)


def mixer_update_kernel(ids_ref, squares_ref, weight_ref, dir_ref, *refs):
    ins, (new_ref, copy_ref, *outs, done_ref) = refs[:6], refs[6:]
    done_ref[...] = jnp.zeros_like(done_ref)
    new_weights(ratio_of(squares_ref, ids_ref[MIXER_ROLE]), weight_ref, dir_ref, new_ref, copy_ref)
    for ref, out in zip(ins, outs, strict=True):
        out[...] = ref[...]


def last_update_kernel(
    ids_ref, squares_ref, mlp_ref, mlp_dir, weight_ref, dir_ref, order_ref,
    mlp_new, mlp_copy, new_ref, copy_ref, norms_ref, ratios_ref,
):
    norms = jnp.sqrt(squares_ref[0:2, :])
    ratios = norms[0:1] / (norms[1:2] + 1e-06)
    norms_ref[...] = norms[:, : norms_ref.shape[1]]
    ratios_ref[...] = ratios[:, : ratios_ref.shape[1]]
    new_weights(ratio_of(squares_ref, ROLES + ids_ref[MLP_ROLE]), mlp_ref, mlp_dir, mlp_new, mlp_copy)
    count = weight_ref.shape[1]
    place = ids_ref[DEVICE] * count + lax.broadcasted_iota(jnp.int32, (1, count), 1)
    first, second, third, fourth = (ratio_of(squares_ref, ROLES + 2 + k) for k in range(4))
    ratio = jnp.where(
        place < 2 * D, jnp.where(place < D, first, second), jnp.where(place < 2 * D + H, third, fourth)
    )
    new_weights(ratio, weight_ref, dir_ref, new_ref, copy_ref)


SMEM = pl.BlockSpec(memory_space=pltpu.SMEM)
ANY = pl.BlockSpec(memory_space=pl.ANY)
VMEM = pl.BlockSpec(memory_space=pltpu.VMEM)


def shape(*dims, dtype=f32):
    return jax.ShapeDtypeStruct(dims, dtype)


def near(*dims, dtype=f32):
    return pltpu.VMEM(dims, dtype)


def kept(value):
    return pltpu.with_memory_space_constraint(value, pltpu.VMEM)


def away(value):
    return pltpu.with_memory_space_constraint(value, pltpu.HBM)


def call(kernel, name, out_shape, *args, order=(), far=(), scratch=(), mib=8):
    in_specs = [SMEM if arg.dtype == jnp.int32 else VMEM for arg in args] + [ANY] * (len(far) + len(order))
    return pl.pallas_call(
        kernel,
        in_specs=in_specs,
        out_specs=jax.tree.map(lambda _: VMEM, out_shape),
        out_shape=out_shape,
        scratch_shapes=list(scratch),
        compiler_params=pltpu.CompilerParams(vmem_limit_bytes=mib * 1024 * 1024),
        name=name,
    )(*[arg if arg.dtype == jnp.int32 else kept(arg) for arg in args], *[away(arg) for arg in far], *order)


def exchange_lane(value, second):
    seqs, batches = lax.axis_size("seq"), lax.axis_size("batch")
    pairs = []
    for s in range(seqs):
        for b in range(batches):
            over_x = (b % 2 == 0) != second
            pairs.append((s * batches + b, (s ^ 1) * batches + b if over_x else s * batches + (b ^ 2)))
    return lax.ppermute(value, AXES, pairs)


def exchange_z_lane(value, second):
    seqs, batches = lax.axis_size("seq"), lax.axis_size("batch")
    pairs = []
    for s in range(seqs):
        for b in range(batches):
            bit = 2 if (b % 2 == 0) != second else 4
            pairs.append((s * batches + b, (s ^ bit) * batches + b))
    return lax.ppermute(value, AXES, pairs)


def after(value, *others):
    return lax.optimization_barrier((value, *others))[0]


def over_z(shard):
    return [shard] + [exchange(shard, 2 * k, 0) for k in range(1, 4)]


def z_terms(sends):
    return [exchange(sent, 2 * (k + 1), 0) for k, sent in enumerate(sends)]


def all_sum(value):
    seqs, batches = lax.axis_size("seq"), lax.axis_size("batch")
    bit = 1
    while bit < batches:
        value = value + exchange(value, 0, bit)
        bit *= 2
    bit = 1
    while bit < seqs:
        value = value + exchange(value, bit, 0)
        bit *= 2
    return value


def relay(ids, total, forward, flipped, beside, hold=()):
    group, before, bit = total, [], 1
    joint = near(4, H)
    if flipped:
        other = exchange(group, 1, 0)
        order = beside[1](group) if 1 in beside else []
        pair, before = call(
            functools.partial(relay_kernel, 1, forward, True), "relay_near", [joint, joint], ids, group, other, order=order
        )
        others = [exchange(pair, 2 * k, 0) for k in range(1, ROLES)]
        order = beside[2](pair) if 2 in beside else []
        return call(
            functools.partial(relay_far_kernel, forward), "relay_far", near(2, H), ids, before, pair, *others, order=order
        )
    while bit < lax.axis_size("seq"):
        last = 2 * bit == lax.axis_size("seq")
        other = exchange(group, bit, 0)
        order = beside[bit](group) if bit in beside else []
        got = call(
            functools.partial(relay_kernel, bit, forward, flipped and bit == 1),
            f"relay_{bit}", near(2, H) if last else [joint, joint],
            ids, group, other, *before, *hold, order=order,
        )
        if not last:
            group, before = got[0], [got[1]]
        bit *= 2
    return got


def flip_by(value, axis, bit):
    return jnp.where(bit == 1, jnp.flip(value, axis), value)


def moments(weight, gradient, first_moment, second, decay_rate):
    first_new = first_decay * first_moment + (1.0 - first_decay) * gradient
    second_new = second_decay * second + (1.0 - second_decay) * gradient * gradient
    direction = (
        first_new
        / (1.0 - first_decay**STEP)
        / (jnp.sqrt(second_new / (1.0 - second_decay**STEP)) + moment_eps)
        + decay_rate * weight
    )
    return (first_new, second_new, direction)


def on_device(
    tokens, doc_lengths, cotangent, mixer_weights, mlp_weights, small_params,
    mixer_first, mixer_second, mlp_first, mlp_second, small_first, small_second,
):
    seqs, batches = lax.axis_size("seq"), lax.axis_size("batch")
    seq_at, batch_at = lax.axis_index("seq"), lax.axis_index("batch")
    device = seq_at * batches + batch_at
    streams, block, _ = tokens.shape
    rows = streams * block
    direct = (seqs, batches) == (8, 4)
    if direct:
        z, x, y, c = seq_at // 2, seq_at % 2, batch_at // 2, batch_at % 2
    else:
        z = x = y = c = jnp.zeros((), jnp.int32)
    mixer_role = device * mixer_weights.shape[0] // H
    mlp_role = device * mlp_weights.shape[0] // FF
    ids = jnp.stack([z, x, y, c, seq_at, device, mixer_role, mlp_role]).astype(jnp.int32)

    slab = shape(ROLES, ROWS, D, dtype=bf16)
    if direct:
        pair_of = near(2, ROWS, D, dtype=bf16)
        count = small_params.shape[0]
        packed = call(
            pack_kernel, "mixer_pack", near(ROWS + TAIL, D, dtype=bf16),
            ids, mixer_weights.astype(bf16), exchange(small_params, 0, 1)[None], far=[small_params[None]],
            scratch=[pltpu.VMEM((1, count), f32), pltpu.SemaphoreType.DMA(())],
        )
        mixer_two = call(
            stack_kernel, "mixer_pair", near(2, ROWS + TAIL, D, dtype=bf16), packed, exchange_z_lane(packed, False)
        )
        mixer_far = exchange_z_lane(mixer_two, True)
        mlp_low = after(mlp_weights, packed).astype(bf16)
        mlp_two = call(stack_kernel, "mlp_pair", pair_of, mlp_low, exchange_lane(mlp_low, False))
        mlp_plane = call(stack_kernel, "mlp_plane", slab, mlp_two, exchange_lane(mlp_two, True))
        gate_slab = call(
            slab_kernel, "mixer_slab", shape(ROLES * ROWS + TAIL, D, dtype=bf16),
            ids, mixer_two, mixer_far, order=[mlp_plane], scratch=[pltpu.VMEM((TAIL, D), f32)],
        )
        mixer_own = [gate_slab] + [exchange(gate_slab, *bits) for bits in PLANE_BITS[1:]]
        mlp_plane = after(mlp_plane, gate_slab)
        mlp_early = call(
            stack_kernel, "mlp_early", shape(2, PLANES, ROWS, D, dtype=bf16), mlp_plane, exchange_z_lane(mlp_plane, False)
        )
        mlp_late = exchange_z_lane(mlp_early, True)
    else:
        small_used = lax.all_gather(small_params.astype(bf16), AXES, axis=0, tiled=True).astype(f32)

        def gathered(shard):
            full = lax.all_gather(shard.astype(bf16), AXES, axis=0, tiled=True)
            return full.reshape(ROLES, PLANES, 2, ROWS, D)

        full = gathered(mixer_weights)
        mixer_own, mixer_par = [[full[:, p, k].reshape(ROLES * ROWS, D) for p in range(PLANES)] for k in range(2)]
        full = gathered(mlp_weights)
        orders = (jnp.array([0, 1, 2, 3]), jnp.array([0, 2, 1, 3]))
        mlp_parts = [full[orders[k], :, k][at] for k in range(2) for at in (slice(0, 2), slice(2, 4))]

    restart, valid = call(marks_kernel, "marks", [shape(rows, 1), shape(rows, 1)], ids, doc_lengths)
    d_out = call(dout_kernel, "d_out", near(rows, D, dtype=bf16), cotangent, valid)

    wide = near(rows, HALF)
    natural = shape(streams, block, D, dtype=bf16)
    low_wide = near(rows, HALF, dtype=bf16)
    low_rows = near(rows, D, dtype=bf16)
    ends = near(2 * SEG, HALF)
    projections = [pltpu.VMEM((rows, HALF), f32)] * 3

    if direct:
        mixer_own = [gate_slab, *after(tuple(mixer_own[1:]), mlp_early, restart, d_out)]
        mixer_par = [exchange(part, 0, 1) for part in mixer_own]
    wide_two, gate_weights = near(2, rows, HALF), near(GATES, HALF, D, dtype=bf16)
    if direct:
        normed, gain_one, gain_two, fb_o, fb_p, ib_o, ib_p, weights_o, both_o, tot_o, sega_o, segb_o = call(
            lambda *refs: scan_first_kernel(count, *refs), "scan_own",
            [low_rows] + [near(1, D)] * 2 + [near(1, HALF)] * 4 + [gate_weights, wide_two, near(4, HALF), ends, ends],
            ids, tokens, restart, *mixer_own,
            scratch=projections + [pltpu.VMEM((4 * SEG, ROWS), f32), pltpu.VMEM((3 * SEG, ROWS), f32)],
        )
    else:
        gain_one, gain_two = small_used[:D][None], small_used[D : 2 * D][None]
        biases = small_used[2 * D :].reshape(2, PLANES, 2, ROWS).transpose(0, 2, 1, 3).reshape(4, 1, HALF)
        fb_o, fb_p, ib_o, ib_p = [biases[k] for k in range(4)]
        normed = call(normed_kernel, "first_norm", low_rows, tokens, gain_one)
        weights_o, both_o, tot_o, sega_o, segb_o = call(
            lambda *refs: scan_kernel(True, *refs), "scan_own", [gate_weights, wide_two, near(4, HALF), ends, ends],
            normed, restart, fb_o, ib_o, *mixer_own, scratch=projections,
        )
    weights_p, both_p, tot, sega_p, segb_p = call(
        lambda *refs: scan_kernel(False, *refs), "scan_other", [gate_weights, wide_two, near(4, H), ends, ends],
        normed, restart, fb_p, ib_p, tot_o, *mixer_par, scratch=projections,
    )

    kept_terms = {}

    def terms_own(ready):
        kept_terms["own"] = call(
            terms_kernel, "terms_own", [wide] * 4,
            normed, fb_o, ib_o, weights_o, order=[ready], scratch=projections[:2],
        )
        return [kept_terms["own"][0]]

    def terms_other(ready):
        kept_terms["other"] = call(
            terms_kernel, "terms_other", [wide] * 4,
            normed, fb_p, ib_p, weights_p, order=[ready], scratch=projections[:2],
        )
        return [kept_terms["other"][0]]

    incoming = relay(ids, tot, True, direct, {1: terms_own, 2: terms_other})
    if direct:
        mlp_late = after(mlp_late, incoming)
        mlp_parts = [mlp_early, mlp_late, exchange(mlp_early, 0, 1), exchange(mlp_late, 0, 1)]

    states_o, states_p, low_o, low_p, resid, normed_two, out_weights = call(
        states_kernel, "states",
        [wide, wide, low_wide, low_wide, near(rows, D), low_rows, near(1, H, D, dtype=bf16)],
        incoming, tokens, gain_two, both_o, both_p, sega_o, sega_p, segb_o, segb_p,
        *mixer_own, *mixer_par,
    )

    terms, half_terms_two = near(PLANES, ROLES, ROWS, D, dtype=bf16), near(2, ROLES, ROWS, D, dtype=bf16)
    d_resid, d_gain_two, mlp_gown, mlp_gnear, mlp_gfar, mlp_act, mlp_held = call(
        mlp_kernel, "mlp",
        [
            near(rows, D), near(1, D), terms, half_terms_two, half_terms_two, near(2 * PLANES, rows, 2 * ROWS, dtype=bf16),
            near(PLANES, 2, ROLES, ROWS, D, dtype=bf16),
        ],
        ids, normed_two, resid, d_out, gain_two, *mlp_parts, mib=16, scratch=[pltpu.VMEM((rows, D), f32)],
    )

    half_terms = near(PLANES, 1, ROWS, D, dtype=bf16)
    back_o, back_p, tot_back, bseg_o, bseg_p, out_gown, out_gpar = call(
        back_kernel, "back_scan", [wide, wide, near(4, H), ends, ends, half_terms, half_terms],
        d_resid, low_o, low_p, both_o, both_p, sega_o, sega_p, out_weights,
    )

    beside = {}
    if direct:
        mlp_got_far, out_got = exchange(mlp_gfar, 0, 1), exchange(out_gpar, 0, 1)
        mlp_got = exchange(after(mlp_gnear, tot_back), 0, 1)
        two_fives = near(2, ROLES + 1, ROWS, D, dtype=bf16)

        def mlp_pair(ready):
            kept_terms["mlp"] = call(
                mlp_pair_kernel, "mlp_pair_sum", two_fives, ids, mlp_gown, mlp_got_far, out_gown, out_got,
                order=[ready],
            )
            return [kept_terms["mlp"]]

        def mark_pair(ready):
            kept_terms["pair"] = ready
            return []

        beside = {1: mlp_pair, 2: mark_pair}

    arriving = relay(ids, tot_back, False, direct, beside)
    terms_o, terms_p = kept_terms["own"], kept_terms["other"]
    if direct:
        mlp_round = exchange_lane(after(kept_terms["mlp"], kept_terms["pair"]), True)

    def gates_back(column, back, sega, bseg, share, df, di, cand, retain, states, order, name):
        return call(
            lambda *refs: gates_kernel(column, *refs), name,
            [near(PLANES, GATES, ROWS, D, dtype=bf16), low_wide, low_wide, low_wide, near(1, HALF), near(1, HALF)],
            arriving, incoming, back, sega, bseg, share, df, di, cand, retain, states, restart, normed, order=order,
        )

    gate_gpar, pf_p, pi_p, pc_p, dfb_p, dib_p = gates_back(
        HALF, back_p, sega_p, bseg_p, *terms_p, both_p, states_p, [tot_back], "gates_other"
    )
    gate_gown, pf_o, pi_o, pc_o, dfb_o, dib_o = gates_back(
        0, back_o, sega_o, bseg_o, *terms_o, both_o, states_o, [dfb_p], "gates_own"
    )

    d_normed, small_terms = call(
        input_terms_kernel, "input_terms", [near(rows, D), near(TAIL, D)],
        ids, tokens, d_gain_two, dfb_o, dfb_p, dib_o, dib_p,
        pf_o, pi_o, pc_o, pf_p, pi_p, pc_p, weights_o, weights_p, order=[dfb_o],
        scratch=[pltpu.VMEM((3 * SEG, ROWS), f32)],
    )

    def token_outputs(ready):
        return call(
            outputs_kernel, "outputs", [natural, natural, near(SEG, ROWS)],
            tokens, gain_one, d_resid, d_normed, resid, valid, mlp_act, mlp_held, order=[ready],
        )

    def with_moments(keep, got, weight, first_moment, second, name):
        count = weight.shape[0]
        return call(
            moments_kernel, name, [shape(count, D)] * 3 + [near(count, D)] + [near(SEG, 128)] * 2,
            keep, got, weight, first_moment, second,
        )

    if direct:
        shard, low_shard = near(ROWS, D), near(ROWS, D, dtype=bf16)
        long, low_long = near(ROWS + TAIL, D), near(ROWS + TAIL, D, dtype=bf16)
        quarter, low_shard = near(2, 2, ROWS, D, dtype=bf16), near(ROWS, D, dtype=bf16)
        small_got = exchange(small_terms, 0, 1)
        mlp_keep, mlp_send, out_keep, out_send = call(
            half_sum_kernel, "mlp_half_sum", [quarter, quarter, low_shard, low_shard], ids,
            mlp_gown, mlp_got, out_gown, out_got, mlp_round, order=[small_got],
        )
        gate_parts = call(
            gate_pair_kernel, "gate_pair_sum", [near(GATES * ROWS + TAIL, D, dtype=bf16)] * PLANES,
            gate_gown, exchange(gate_gpar, 0, 1), small_terms, small_got, order=[out_keep],
        )
        gate_round = [gate_parts[0]] + [
            exchange(part, *bits) for part, bits in zip(gate_parts[1:], PLANE_BITS[1:], strict=True)
        ]
        d_x, output, x_done = token_outputs(gate_parts[0])
        out_got = exchange_lane(out_send, False)
        two = near(2, ROWS, D, dtype=bf16)
        mlp_stay, mlp_send = call(
            mlp_far_kernel, "mlp_z_sum", [two, two], mlp_keep, exchange_z_lane(mlp_send, False)
        )
        mlp_stay, mlp_send = call(
            mlp_last_kernel, "mlp_z_last", [shard, low_shard], mlp_stay, exchange_z_lane(mlp_send, True)
        )
        mlp_done = with_moments(
            mlp_stay, exchange_lane(mlp_send, False), mlp_weights, mlp_first, mlp_second, "mlp_moments"
        )
        gate_keep, *gate_sends = call(
            gate_plane_kernel, "gate_plane_sum", [long] + [low_long] * 3, ids, *gate_round, out_keep, out_got,
            order=[x_done],
        )
        gate_got = z_terms(gate_sends)
    else:

        def scattered(own, par):
            full_terms = jnp.stack([own, par]).transpose(2, 1, 0, 3, 4).reshape(-1, D)
            return lax.psum_scatter(full_terms.astype(f32), AXES, scatter_dimension=0, tiled=True)

        d_x, output, _ = token_outputs(small_terms)
        mlp_grad = scattered(mlp_gown, jnp.concatenate([mlp_gnear, mlp_gfar], axis=0))
        mixer_grad = scattered(
            jnp.concatenate([gate_gown, out_gown], axis=1), jnp.concatenate([gate_gpar, out_gpar], axis=1)
        )
        none = jnp.zeros_like(mlp_grad, dtype=bf16)
        mlp_done = with_moments(mlp_grad, none, mlp_weights, mlp_first, mlp_second, "mlp_moments")
        gate_keep = jnp.concatenate([mixer_grad, lax.psum(small_terms, AXES)], axis=0)
        gate_got = [jnp.zeros_like(gate_keep, dtype=bf16)] * 3
    mlp_grad, mlp_first_new, mlp_second_new, mlp_dir, mlp_wsum, mlp_dsum = mlp_done
    count, mixer_count = small_params.shape[0], mixer_weights.shape[0]
    line, matrix = shape(1, count), shape(mixer_count, D)
    mixer_grad, mixer_first_new, mixer_second_new, mixer_dir, small_grad, small_first_new, small_second_new, small_dir, squares = call(
        finish_kernel, "finish", [near(mixer_count, D)] * 4 + [near(1, count)] * 4 + [near(SEG, ROWS)],
        ids, gate_keep, *gate_got, mlp_wsum, mlp_dsum, mixer_weights, mixer_first, mixer_second,
        small_params[None], small_first[None], small_second[None], scratch=[pltpu.VMEM((4 * SEG, ROWS), f32)],
    )

    def mixer_update(sums):
        matrix = shape(mixer_count, D)
        return call(
            mixer_update_kernel, "mixer_update", [matrix, shape(mixer_count, D, dtype=bf16)] + [matrix] * 3 + [line] * 3 + [near(SEG, ROWS)],
            ids, sums, mixer_weights, mixer_dir, mixer_grad, mixer_first_new, mixer_second_new,
            small_grad, small_first_new, small_second_new,
        )

    if direct:
        sums = squares + exchange(squares, 0, 1)
        over_y, over_x, over_both = (exchange(sums, *bits) for bits in PLANE_BITS[1:])
        sums = (sums + over_y) + (over_x + over_both)
        stored = mixer_update(sums)
        near_z, far_z, both_z = (exchange(sums, 2 * k, 0) for k in range(1, ROLES))
        sums = (sums + near_z) + (far_z + both_z)
    else:
        sums = all_sum(squares)
        stored = mixer_update(sums)
    mixer_new, mixer_copy, mixer_grad, mixer_first_new, mixer_second_new, *stored = stored
    small_grad, small_first_new, small_second_new, mixer_updated = stored
    matrix, low_line = shape(*mlp_weights.shape), shape(1, count, dtype=bf16)
    mlp_new, mlp_copy, small_new, small_copy, tensor_norms, trust_ratios = call(
        last_update_kernel, "last_update",
        [matrix, shape(*mlp_weights.shape, dtype=bf16), line, low_line, shape(2, 10), shape(1, 10)],
        ids, sums, mlp_weights, mlp_dir, small_params[None], small_dir, order=[mixer_updated],
    )
    return (
        output,
        d_x,
        mixer_grad,
        mlp_grad,
        small_grad[0],
        mixer_first_new,
        mixer_second_new,
        mlp_first_new,
        mlp_second_new,
        small_first_new[0],
        small_second_new[0],
        mixer_new,
        mlp_new,
        small_new[0],
        mixer_copy,
        mlp_copy,
        small_copy[0],
        tensor_norms,
        trust_ratios[0],
    )


def solution(mesh):
    shard = P(("seq", "batch"), None)
    shard_flat = P(("seq", "batch"))
    stream = P("batch", "seq", None)
    return jax.shard_map(
        on_device,
        mesh=mesh,
        in_specs=(
            stream, P("batch", None), stream, shard, shard, shard_flat,
            shard, shard, shard, shard, shard_flat, shard_flat,
        ),
        out_specs=(
            stream, stream, shard, shard, shard_flat, shard, shard, shard, shard, shard_flat, shard_flat,
            shard, shard, shard_flat, shard, shard, shard_flat, P(), P(),
        ),
        check_vma=False,
    )
```

profile of v0, /device:TPU:0, one launch (start us, length us, event | category | flops | bytes accessed | tf_op | source)
XLA Modules:
  0.0 158.4 jit_solution(9314119013576163387)
XLA Ops:
  3.5 2.8 %collective-permute-start.1 = (bf16[144,512]{1,0:T(8,128)(2,1)S(1)}, bf16[144,512]{1,0:T(8,128)(2,1)S(1)}, u32[]{:S(2)}, u32[]{:S(2)}) collective-permute-start(bf16[144,512]{1,0:T(8,128)(2,1)S(1)} %mixer_pack.1.first_ref), channel_id=1, source_target_pairs={{0,8},{1,17},{2,10},{3,19},{4,12},{5,21},{6,14},{7,23},{8,0},{9,25... | collective-permute-start | bytes 442376 | tf_op jit(solution)/shard_map/ppermute | solution.py:749
  8.8 1.8 %collective-permute-done.1.second_ref = bf16[144,512]{1,0:T(8,128)(2,1)S(1)} collective-permute-done((bf16[144,512]{1,0:T(8,128)(2,1)S(1)}, bf16[144,512]{1,0:T(8,128)(2,1)S(1)}, u32[]{:S(2)}, u32[]{:S(2)}) %collective-permute-start.1) | collective-permute-done | bytes 147488 | tf_op jit(solution)/shard_map/ppermute | solution.py:749
  10.6 2.8 %collective-permute-start.2 = (bf16[2,144,512]{2,1,0:T(8,128)(2,1)S(1)}, bf16[2,144,512]{2,1,0:T(8,128)(2,1)S(1)}, u32[]{:S(2)}, u32[]{:S(2)}) collective-permute-start(bf16[2,144,512]{2,1,0:T(8,128)(2,1)S(1)} %mixer_pair.1.early_ref), channel_id=1, source_target_pairs={{0,16},{1,9},{2,18},{3,11},{4,20},{5,13},{6,22},{7,15},{8,24},{9,1... | collective-permute-start | bytes 884744 | tf_op jit(solution)/shard_map/ppermute | solution.py:749
  13.4 1.6 %collective-permute-start.4 = (bf16[2,128,512]{2,1,0:T(8,128)(2,1)S(1)}, bf16[2,128,512]{2,1,0:T(8,128)(2,1)S(1)}, u32[]{:S(2)}, u32[]{:S(2)}) collective-permute-start(bf16[2,128,512]{2,1,0:T(8,128)(2,1)S(1)} %mlp_pair.1.first_ref), channel_id=1, source_target_pairs={{0,2},{1,5},{2,0},{3,7},{4,6},{5,1},{6,4},{7,3},{8,10},{9,13},{10,... | collective-permute-start | bytes 786440 | tf_op jit(solution)/shard_map/ppermute | solution.py:739
  15.0 4.9 %collective-permute-done.4.second_ref = bf16[2,128,512]{2,1,0:T(8,128)(2,1)S(1)} collective-permute-done((bf16[2,128,512]{2,1,0:T(8,128)(2,1)S(1)}, bf16[2,128,512]{2,1,0:T(8,128)(2,1)S(1)}, u32[]{:S(2)}, u32[]{:S(2)}) %collective-permute-start.4) | collective-permute-done | bytes 262176 | tf_op jit(solution)/shard_map/ppermute | solution.py:739
  20.7 2.9 %collective-permute-start.8 = (bf16[4,128,512]{2,1,0:T(8,128)(2,1)S(1)}, bf16[4,128,512]{2,1,0:T(8,128)(2,1)S(1)}, u32[]{:S(2)}, u32[]{:S(2)}) collective-permute-start(bf16[4,128,512]{2,1,0:T(8,128)(2,1)S(1)} %mlp_plane.1.refs_0_.first_ref), channel_id=1, source_target_pairs={{0,8},{1,17},{2,10},{3,19},{4,12},{5,21},{6,14},{7,23},{8,0},{9,25... | collective-permute-start | bytes 1572872 | tf_op jit(solution)/shard_map/ppermute | solution.py:749
  23.5 2.4 %collective-permute-start.7 = (bf16[528,512]{1,0:T(8,128)(2,1)S(1)}, bf16[528,512]{1,0:T(8,128)(2,1)S(1)}, u32[]{:S(2)}, u32[]{:S(2)}) collective-permute-start(bf16[528,512]{1,0:T(8,128)(2,1)S(1)} %mixer_slab.1.refs_3_.refs_0_), channel_id=1, source_target_pairs={{0,6},{1,7},{2,4},{3,5},{4,2},{5,3},{6,0},{7,1},{8,14},{9,15},{10,... | collective-permute-start | bytes 1622024 | tf_op jit(solution)/shard_map/ppermute | solution.py:57
  27.0 9.2 %collective-permute-done.8.second_ref = bf16[4,128,512]{2,1,0:T(8,128)(2,1)S(1)} collective-permute-done((bf16[4,128,512]{2,1,0:T(8,128)(2,1)S(1)}, bf16[4,128,512]{2,1,0:T(8,128)(2,1)S(1)}, u32[]{:S(2)}, u32[]{:S(2)}) %collective-permute-start.8) | collective-permute-done | bytes 524320 | tf_op jit(solution)/shard_map/ppermute | solution.py:749
  39.7 9.8 %collective-permute-done.6.refs_5_.refs_2_ = bf16[528,512]{1,0:T(8,128)(2,1)S(1)} collective-permute-done((bf16[528,512]{1,0:T(8,128)(2,1)S(1)}, bf16[528,512]{1,0:T(8,128)(2,1)S(1)}, u32[]{:S(2)}, u32[]{:S(2)}) %collective-permute-start.6) | collective-permute-done | bytes 540704 | tf_op jit(solution)/shard_map/ppermute | solution.py:57
  50.0 2.5 %scan_own.1 = (bf16[512,512]{1,0:T(8,128)(2,1)S(1)}, f32[1,512]{1,0:T(1,128)S(1)}, f32[1,512]{1,0:T(1,128)S(1)}, f32[1,512]{1,0:T(1,128)S(1)}, f32[1,512]{1,0:T(...) custom-call(s32[8]{0:T(128)S(1)} %stack.35.ids_ref.refs_0_, ...), custom_call_target="tpu_custom_call" | custom-call | tf_op jit(solution)/shard_map/scan_own/pallas_call | solution.py:721
  53.0 1.7 %scan_other.1 = (bf16[3,512,512]{2,1,0:T(8,128)(2,1)S(1)}, f32[2,512,512]{2,1,0:T(8,128)S(1)}, f32[4,1024]{1,0:T(4,128)S(1)}, f32[16,512]{1,0:T(8,128)S(1)}, f32[16,512]{1,0:T(8,128)S(1)}) custom-call(bf16[512,512]{1,0:T(8,128)(2,1)S(1)} %get-tuple-element.150.refs_0_.normed_ref.refs_12_, f32[512,1]{1,0:T(8,128)S(1)} %get-tuple-element.142.refs_2_.refs_1_.refs_11_, ...), custom_call_target="tpu_custom_call" | custom-call | tf_op jit(solution)/shard_map/scan_other/pallas_call | solution.py:721
  56.2 2.1 %terms_own.1 = (f32[512,512]{1,0:T(8,128)S(1)}, f32[512,512]{1,0:T(8,128)S(1)}, f32[512,512]{1,0:T(8,128)S(1)}, f32[512,512]{1,0:T(8,128)S(1)}) custom-call(bf16[512,512]{1,0:T(8,128)(2,1)S(1)} %get-tuple-element.150.refs_0_.normed_ref.refs_12_, f32[1,512]{1,0:T(1,128)S(1)} %get-tuple-element.155.fb_ref, f32[1,512]{1,0:T(1,128)S(1)} %get-tuple-element.156.ib_ref, ...), custom_call_target="tpu_custom_call" | custom-call | tf_op jit(solution)/shard_map/terms_own/pallas_call | solution.py:721
  59.4 1.7 %collective-permute-start.15 = (f32[4,1024]{1,0:T(4,128)S(1)}, f32[4,1024]{1,0:T(4,128)S(1)}, u32[]{:S(2)}, u32[]{:S(2)}) collective-permute-start(f32[4,1024]{1,0:T(4,128)S(1)} %get-tuple-element.160.refs_0_), channel_id=1, source_target_pairs={{0,16},{1,17},{2,18},{3,19},{4,20},{5,21},{6,22},{7,23},{8,24},{9,... | collective-permute-start | bytes 49160 | tf_op jit(solution)/shard_map/ppermute | solution.py:57
  61.0 2.5 %collective-permute-start.14 = (f32[4,1024]{1,0:T(4,128)S(1)}, f32[4,1024]{1,0:T(4,128)S(1)}, u32[]{:S(2)}, u32[]{:S(2)}) collective-permute-start(f32[4,1024]{1,0:T(4,128)S(1)} %get-tuple-element.160.refs_0_), channel_id=1, source_target_pairs={{0,8},{1,9},{2,10},{3,11},{4,12},{5,13},{6,14},{7,15},{8,0},{9,1},... | collective-permute-start | bytes 49160 | tf_op jit(solution)/shard_map/ppermute | solution.py:57
  63.5 2.3 %terms_other.1 = (f32[512,512]{1,0:T(8,128)S(1)}, f32[512,512]{1,0:T(8,128)S(1)}, f32[512,512]{1,0:T(8,128)S(1)}, f32[512,512]{1,0:T(8,128)S(1)}) custom-call(bf16[512,512]{1,0:T(8,128)(2,1)S(1)} %get-tuple-element.150.refs_0_.normed_ref.refs_12_, f32[1,512]{1,0:T(1,128)S(1)} %get-tuple-element.151.refs_2_.fb_ref, ...), custom_call_target="tpu_custom_call" | custom-call | tf_op jit(solution)/shard_map/terms_other/pallas_call | solution.py:721
  69.3 7.2 %mlp.1 = (f32[512,512]{1,0:T(8,128)S(1)}, f32[1,512]{1,0:T(1,128)S(1)}, bf16[4,4,128,512]{3,2,1,0:T(8,128)(2,1)S(1)}, bf16[2,4,128,512]{3,2,1,0:T(8,128)(2,1)S(1...) custom-call(s32[8]{0:T(128)S(1)} %stack.35.ids_ref.refs_0_, ...), custom_call_target="tpu_custom_call" | custom-call | tf_op jit(solution)/shard_map/mlp/pallas_call | solution.py:721
  84.4 1.6 %collective-permute-start.25 = (f32[4,1024]{1,0:T(4,128)S(1)}, f32[4,1024]{1,0:T(4,128)S(1)}, u32[]{:S(2)}, u32[]{:S(2)}) collective-permute-start(f32[4,1024]{1,0:T(4,128)S(1)} %get-tuple-element.184.refs_0_), channel_id=1, source_target_pairs={{0,24},{1,25},{2,26},{3,27},{4,28},{5,29},{6,30},{7,31},{8,16},{9,... | collective-permute-start | bytes 49160 | tf_op jit(solution)/shard_map/ppermute | solution.py:57
  87.1 1.7 %collective-permute-start.23 = (f32[4,1024]{1,0:T(4,128)S(1)}, f32[4,1024]{1,0:T(4,128)S(1)}, u32[]{:S(2)}, u32[]{:S(2)}) collective-permute-start(f32[4,1024]{1,0:T(4,128)S(1)} %get-tuple-element.184.refs_0_), channel_id=1, source_target_pairs={{0,8},{1,9},{2,10},{3,11},{4,12},{5,13},{6,14},{7,15},{8,0},{9,1},... | collective-permute-start | bytes 49160 | tf_op jit(solution)/shard_map/ppermute | solution.py:57
  91.4 1.7 %gates_other.1 = (bf16[4,3,128,512]{3,2,1,0:T(8,128)(2,1)S(1)}, bf16[512,512]{1,0:T(8,128)(2,1)S(1)}, bf16[512,512]{1,0:T(8,128)(2,1)S(1)}, bf16[512,512]{1,0:T(...) custom-call(f32[2,1024]{1,0:T(2,128)S(1)} %relay_far.3.refs_0_, f32[2,1024]{1,0:T(2,128)S(1)} %relay_far.2.inc_ref.refs_1_, ...), custom_call_target="tpu_custom_call" | custom-call | tf_op jit(solution)/shard_map/gates_other/pallas_call | solution.py:721
  93.6 1.7 %gates_own.1 = (bf16[4,3,128,512]{3,2,1,0:T(8,128)(2,1)S(1)}, bf16[512,512]{1,0:T(8,128)(2,1)S(1)}, bf16[512,512]{1,0:T(8,128)(2,1)S(1)}, bf16[512,512]{1,0:T(8,...) custom-call(f32[2,1024]{1,0:T(2,128)S(1)} %relay_far.3.refs_0_, f32[2,1024]{1,0:T(2,128)S(1)} %relay_far.2.inc_ref.refs_1_, ...), custom_call_target="tpu_custom_call" | custom-call | tf_op jit(solution)/shard_map/gates_own/pallas_call | solution.py:721
  95.3 2.8 %input_terms.1 = (f32[512,512]{1,0:T(8,128)S(1)}, f32[16,512]{1,0:T(8,128)S(1)}) custom-call(s32[8]{0:T(128)S(1)} %stack.35.ids_ref.refs_0_, bf16[2,256,512]{2,1,0:T(8,128)(2,1)S(1)} %copy-done, f32[1,512]{1,0:T(1,128)S(1)} %get-tuple-element.174.dgain_two_ref, f32[1,512]{1,0:T(1,128)S(1)} %get-tuple-element.198.dfb_o.refs_8_, ...), custom_call_target="tpu_custom_call" | custom-call | tf_op jit(solution)/shard_map/input_terms/pallas_call | solution.py:721
  106.8 8.6 %collective-permute-done.37.got_ref = bf16[2,2,128,512]{3,2,1,0:T(8,128)(2,1)S(1)} collective-permute-done((bf16[2,2,128,512]{3,2,1,0:T(8,128)(2,1)S(1)}, bf16[2,2,128,512]{3,2,1,0:T(8,128)(2,1)S(1)}, u32[]{:S(2)}, u32[]{:S(2)}) %collective-permute-start.37) | collective-permute-done | bytes 524320 | tf_op jit(solution)/shard_map/ppermute | solution.py:749
  115.5 1.7 %collective-permute-start.38 = (bf16[2,128,512]{2,1,0:T(8,128)(2,1)S(1)}, bf16[2,128,512]{2,1,0:T(8,128)(2,1)S(1)}, u32[]{:S(2)}, u32[]{:S(2)}) collective-permute-start(bf16[2,128,512]{2,1,0:T(8,128)(2,1)S(1)} %get-tuple-element.232), channel_id=1, source_target_pairs={{0,16},{1,9},{2,18},{3,11},{4,20},{5,13},{6,22},{7,15},{8,24},{9,1... | collective-permute-start | bytes 786440 | tf_op jit(solution)/shard_map/ppermute | solution.py:749
  118.7 3.0 %outputs.1 = (bf16[2,256,512]{2,1,0:T(8,128)(2,1)}, bf16[2,256,512]{2,1,0:T(8,128)(2,1)}, f32[8,128]{1,0:T(8,128)S(1)}) custom-call(bf16[2,256,512]{2,1,0:T(8,128)(2,1)S(1)} %copy-done, f32[1,512]{1,0:T(1,128)S(1)} %get-tuple-element.149.gain_ref, f32[512,512]{1,0:T(8,128)S(1)} %get-tuple-element.173.dresid_ref, ...), custom_call_target="tpu_custom_call" | custom-call | tf_op jit(solution)/shard_map/outputs/pallas_call | solution.py:721
  121.7 2.8 %collective-permute-done.33.out_got = bf16[128,512]{1,0:T(8,128)(2,1)S(1)} collective-permute-done((bf16[128,512]{1,0:T(8,128)(2,1)S(1)}, bf16[128,512]{1,0:T(8,128)(2,1)S(1)}, u32[]{:S(2)}, u32[]{:S(2)}) %collective-permute-start.33) | collective-permute-done | bytes 131104 | tf_op jit(solution)/shard_map/ppermute | solution.py:739
  126.5 2.0 %collective-permute-start.35 = (bf16[144,512]{1,0:T(8,128)(2,1)S(1)}, bf16[144,512]{1,0:T(8,128)(2,1)S(1)}, u32[]{:S(2)}, u32[]{:S(2)}) collective-permute-start(bf16[144,512]{1,0:T(8,128)(2,1)S(1)} %get-tuple-element.227), channel_id=1, source_target_pairs={{0,16},{1,17},{2,18},{3,19},{4,20},{5,21},{6,22},{7,23},{8,24},{9,... | collective-permute-start | bytes 442376 | tf_op jit(solution)/shard_map/ppermute | solution.py:57
  128.4 1.6 %collective-permute-start.36 = (bf16[144,512]{1,0:T(8,128)(2,1)S(1)}, bf16[144,512]{1,0:T(8,128)(2,1)S(1)}, u32[]{:S(2)}, u32[]{:S(2)}) collective-permute-start(bf16[144,512]{1,0:T(8,128)(2,1)S(1)} %get-tuple-element.228), channel_id=1, source_target_pairs={{0,24},{1,25},{2,26},{3,27},{4,28},{5,29},{6,30},{7,31},{8,16},{9,... | collective-permute-start | bytes 442376 | tf_op jit(solution)/shard_map/ppermute | solution.py:57
  131.7 3.5 %collective-permute-done.39.got_ref = bf16[128,512]{1,0:T(8,128)(2,1)S(1)} collective-permute-done((bf16[128,512]{1,0:T(8,128)(2,1)S(1)}, bf16[128,512]{1,0:T(8,128)(2,1)S(1)}, u32[]{:S(2)}, u32[]{:S(2)}) %collective-permute-start.39) | collective-permute-done | bytes 131104 | tf_op jit(solution)/shard_map/ppermute | solution.py:739
  136.1 4.3 %collective-permute-done.35.g2_ref = bf16[144,512]{1,0:T(8,128)(2,1)S(1)} collective-permute-done((bf16[144,512]{1,0:T(8,128)(2,1)S(1)}, bf16[144,512]{1,0:T(8,128)(2,1)S(1)}, u32[]{:S(2)}, u32[]{:S(2)}) %collective-permute-start.35) | collective-permute-done | bytes 147488 | tf_op jit(solution)/shard_map/ppermute | solution.py:57
  142.9 2.3 %collective-permute-start.43 = (f32[8,128]{1,0:T(8,128)S(1)}, f32[8,128]{1,0:T(8,128)S(1)}, u32[]{:S(2)}, u32[]{:S(2)}) collective-permute-start(f32[8,128]{1,0:T(8,128)S(1)} %add.38), channel_id=1, source_target_pairs={{0,6},{1,7},{2,4},{3,5},{4,2},{5,3},{6,0},{7,1},{8,14},{9,15},{10,... | collective-permute-start | bytes 12296 | tf_op jit(solution)/shard_map/ppermute | solution.py:57
  149.3 1.8 %collective-permute-start.46 = (f32[8,128]{1,0:T(8,128)S(1)}, f32[8,128]{1,0:T(8,128)S(1)}, u32[]{:S(2)}, u32[]{:S(2)}) collective-permute-start(f32[8,128]{1,0:T(8,128)S(1)} %add_add_fusion.1.squares_ref), channel_id=1, source_target_pairs={{0,24},{1,25},{2,26},{3,27},{4,28},{5,29},{6,30},{7,31},{8,16},{9,... | collective-permute-start | bytes 12296 | tf_op jit(solution)/shard_map/ppermute | solution.py:57
  151.1 2.3 %collective-permute-start.45 = (f32[8,128]{1,0:T(8,128)S(1)}, f32[8,128]{1,0:T(8,128)S(1)}, u32[]{:S(2)}, u32[]{:S(2)}) collective-permute-start(f32[8,128]{1,0:T(8,128)S(1)} %add_add_fusion.1.squares_ref), channel_id=1, source_target_pairs={{0,16},{1,17},{2,18},{3,19},{4,20},{5,21},{6,22},{7,23},{8,24},{9,... | collective-permute-start | bytes 12296 | tf_op jit(solution)/shard_map/ppermute | solution.py:57
  (125 shorter events, 56.1 us)
Async XLA Ops:
  3.5 7.1 %collective-permute-start.1 = (bf16[144,512]{1,0:T(8,128)(2,1)S(1)}, bf16[144,512]{1,0:T(8,128)(2,1)S(1)}, u32[]{:S(2)}, u32[]{:S(2)}) collective-permute-start(bf16[144,512]{1,0:T(8,128)(2,1)S(1)} %mixer_pack.1.first_ref), channel_id=1, source_target_pairs={{0,8},{1,17},{2,10},{3,19},{4,12},{5,21},{6,14},{7,23},{8,0},{9,25... | collective-permute-start | bytes 442376 | tf_op jit(solution)/shard_map/ppermute | solution.py:749
  7.3 6.1 %collective-permute-start.3 = (bf16[128,512]{1,0:T(8,128)(2,1)S(1)}, bf16[128,512]{1,0:T(8,128)(2,1)S(1)}, u32[]{:S(2)}, u32[]{:S(2)}) collective-permute-start(bf16[128,512]{1,0:T(8,128)(2,1)S(1)} %convert_element_type.7.first_ref), channel_id=1, source_target_pairs={{0,4},{1,3},{2,6},{3,1},{4,0},{5,7},{6,2},{7,5},{8,12},{9,11},{10,... | collective-permute-start | bytes 393224 | tf_op jit(solution)/shard_map/ppermute | solution.py:739
  10.6 9.4 %collective-permute-start.2 = (bf16[2,144,512]{2,1,0:T(8,128)(2,1)S(1)}, bf16[2,144,512]{2,1,0:T(8,128)(2,1)S(1)}, u32[]{:S(2)}, u32[]{:S(2)}) collective-permute-start(bf16[2,144,512]{2,1,0:T(8,128)(2,1)S(1)} %mixer_pair.1.early_ref), channel_id=1, source_target_pairs={{0,16},{1,9},{2,18},{3,11},{4,20},{5,13},{6,22},{7,15},{8,24},{9,1... | collective-permute-start | bytes 884744 | tf_op jit(solution)/shard_map/ppermute | solution.py:749
  13.4 6.4 %collective-permute-start.4 = (bf16[2,128,512]{2,1,0:T(8,128)(2,1)S(1)}, bf16[2,128,512]{2,1,0:T(8,128)(2,1)S(1)}, u32[]{:S(2)}, u32[]{:S(2)}) collective-permute-start(bf16[2,128,512]{2,1,0:T(8,128)(2,1)S(1)} %mlp_pair.1.first_ref), channel_id=1, source_target_pairs={{0,2},{1,5},{2,0},{3,7},{4,6},{5,1},{6,4},{7,3},{8,10},{9,13},{10,... | collective-permute-start | bytes 786440 | tf_op jit(solution)/shard_map/ppermute | solution.py:739
  20.7 15.6 %collective-permute-start.8 = (bf16[4,128,512]{2,1,0:T(8,128)(2,1)S(1)}, bf16[4,128,512]{2,1,0:T(8,128)(2,1)S(1)}, u32[]{:S(2)}, u32[]{:S(2)}) collective-permute-start(bf16[4,128,512]{2,1,0:T(8,128)(2,1)S(1)} %mlp_plane.1.refs_0_.first_ref), channel_id=1, source_target_pairs={{0,8},{1,17},{2,10},{3,19},{4,12},{5,21},{6,14},{7,23},{8,0},{9,25... | collective-permute-start | bytes 1572872 | tf_op jit(solution)/shard_map/ppermute | solution.py:749
  23.5 16.2 %collective-permute-start.7 = (bf16[528,512]{1,0:T(8,128)(2,1)S(1)}, bf16[528,512]{1,0:T(8,128)(2,1)S(1)}, u32[]{:S(2)}, u32[]{:S(2)}) collective-permute-start(bf16[528,512]{1,0:T(8,128)(2,1)S(1)} %mixer_slab.1.refs_3_.refs_0_), channel_id=1, source_target_pairs={{0,6},{1,7},{2,4},{3,5},{4,2},{5,3},{6,0},{7,1},{8,14},{9,15},{10,... | collective-permute-start | bytes 1622024 | tf_op jit(solution)/shard_map/ppermute | solution.py:57
  26.0 23.5 %collective-permute-start.6 = (bf16[528,512]{1,0:T(8,128)(2,1)S(1)}, bf16[528,512]{1,0:T(8,128)(2,1)S(1)}, u32[]{:S(2)}, u32[]{:S(2)}) collective-permute-start(bf16[528,512]{1,0:T(8,128)(2,1)S(1)} %mixer_slab.1.refs_3_.refs_0_), channel_id=1, source_target_pairs={{0,4},{1,5},{2,6},{3,7},{4,0},{5,1},{6,2},{7,3},{8,12},{9,13},{10,... | collective-permute-start | bytes 1622024 | tf_op jit(solution)/shard_map/ppermute | solution.py:57
  26.5 23.0 %collective-permute-start.5 = (bf16[528,512]{1,0:T(8,128)(2,1)S(1)}, bf16[528,512]{1,0:T(8,128)(2,1)S(1)}, u32[]{:S(2)}, u32[]{:S(2)}) collective-permute-start(bf16[528,512]{1,0:T(8,128)(2,1)S(1)} %mixer_slab.1.refs_3_.refs_0_), channel_id=1, source_target_pairs={{0,2},{1,3},{2,0},{3,1},{4,6},{5,7},{6,4},{7,5},{8,10},{9,11},{10,... | collective-permute-start | bytes 1622024 | tf_op jit(solution)/shard_map/ppermute | solution.py:57
  36.3 30.1 %collective-permute-start.17 = (bf16[2,4,128,512]{3,2,1,0:T(8,128)(2,1)S(1)}, bf16[2,4,128,512]{3,2,1,0:T(8,128)(2,1)S(1)}, u32[]{:S(2)}, u32[]{:S(2)}) collective-permute-start(bf16[2,4,128,512]{3,2,1,0:T(8,128)(2,1)S(1)} %mlp_early.1.refs_0_), channel_id=1, source_target_pairs={{0,16},{1,9},{2,18},{3,11},{4,20},{5,13},{6,22},{7,15},{8,24},{9,1... | collective-permute-start | bytes 3145736 | tf_op jit(solution)/shard_map/ppermute | solution.py:749
  39.1 13.4 %collective-permute-start.9 = (bf16[528,512]{1,0:T(8,128)(2,1)S(1)}, bf16[528,512]{1,0:T(8,128)(2,1)S(1)}, u32[]{:S(2)}, u32[]{:S(2)}) collective-permute-start(bf16[528,512]{1,0:T(8,128)(2,1)S(1)} %mixer_slab.1.refs_3_.refs_0_), channel_id=1, source_target_pairs={{0,1},{1,0},{2,3},{3,2},{4,5},{5,4},{6,7},{7,6},{8,9},{9,8},{10,11... | collective-permute-start | bytes 1622024 | tf_op jit(solution)/shard_map/ppermute | solution.py:57
  59.0 6.8 %collective-permute-start.16 = (f32[4,1024]{1,0:T(4,128)S(1)}, f32[4,1024]{1,0:T(4,128)S(1)}, u32[]{:S(2)}, u32[]{:S(2)}) collective-permute-start(f32[4,1024]{1,0:T(4,128)S(1)} %get-tuple-element.160.refs_0_), channel_id=1, source_target_pairs={{0,24},{1,25},{2,26},{3,27},{4,28},{5,29},{6,30},{7,31},{8,16},{9,... | collective-permute-start | bytes 49160 | tf_op jit(solution)/shard_map/ppermute | solution.py:57
  59.4 6.5 %collective-permute-start.15 = (f32[4,1024]{1,0:T(4,128)S(1)}, f32[4,1024]{1,0:T(4,128)S(1)}, u32[]{:S(2)}, u32[]{:S(2)}) collective-permute-start(f32[4,1024]{1,0:T(4,128)S(1)} %get-tuple-element.160.refs_0_), channel_id=1, source_target_pairs={{0,16},{1,17},{2,18},{3,19},{4,20},{5,21},{6,22},{7,23},{8,24},{9,... | collective-permute-start | bytes 49160 | tf_op jit(solution)/shard_map/ppermute | solution.py:57
  61.0 4.8 %collective-permute-start.14 = (f32[4,1024]{1,0:T(4,128)S(1)}, f32[4,1024]{1,0:T(4,128)S(1)}, u32[]{:S(2)}, u32[]{:S(2)}) collective-permute-start(f32[4,1024]{1,0:T(4,128)S(1)} %get-tuple-element.160.refs_0_), channel_id=1, source_target_pairs={{0,8},{1,9},{2,10},{3,11},{4,12},{5,13},{6,14},{7,15},{8,0},{9,1},... | collective-permute-start | bytes 49160 | tf_op jit(solution)/shard_map/ppermute | solution.py:57
  63.5 4.5 %collective-permute-start.18 = (bf16[2,4,128,512]{3,2,1,0:T(8,128)(2,1)S(1)}, bf16[2,4,128,512]{3,2,1,0:T(8,128)(2,1)S(1)}, u32[]{:S(2)}, u32[]{:S(2)}) collective-permute-start(bf16[2,4,128,512]{3,2,1,0:T(8,128)(2,1)S(1)} %mlp_early.1.refs_0_), channel_id=1, source_target_pairs={{0,1},{1,0},{2,3},{3,2},{4,5},{5,4},{6,7},{7,6},{8,9},{9,8},{10,11... | collective-permute-start | bytes 3145736 | tf_op jit(solution)/shard_map/ppermute | solution.py:57
  82.9 17.7 %collective-permute-start.29 = (bf16[2,5,128,512]{3,2,1,0:T(8,128)(2,1)S(1)}, bf16[2,5,128,512]{3,2,1,0:T(8,128)(2,1)S(1)}, u32[]{:S(2)}, u32[]{:S(2)}) collective-permute-start(bf16[2,5,128,512]{3,2,1,0:T(8,128)(2,1)S(1)} %mlp_pair_sum.1.refs_0_), channel_id=1, source_target_pairs={{0,2},{1,5},{2,0},{3,7},{4,6},{5,1},{6,4},{7,3},{8,10},{9,13},{10,... | collective-permute-start | bytes 3932168 | tf_op jit(solution)/shard_map/ppermute | solution.py:739
  84.4 5.5 %collective-permute-start.25 = (f32[4,1024]{1,0:T(4,128)S(1)}, f32[4,1024]{1,0:T(4,128)S(1)}, u32[]{:S(2)}, u32[]{:S(2)}) collective-permute-start(f32[4,1024]{1,0:T(4,128)S(1)} %get-tuple-element.184.refs_0_), channel_id=1, source_target_pairs={{0,24},{1,25},{2,26},{3,27},{4,28},{5,29},{6,30},{7,31},{8,16},{9,... | collective-permute-start | bytes 49160 | tf_op jit(solution)/shard_map/ppermute | solution.py:57
  86.0 4.6 %collective-permute-start.24 = (f32[4,1024]{1,0:T(4,128)S(1)}, f32[4,1024]{1,0:T(4,128)S(1)}, u32[]{:S(2)}, u32[]{:S(2)}) collective-permute-start(f32[4,1024]{1,0:T(4,128)S(1)} %get-tuple-element.184.refs_0_), channel_id=1, source_target_pairs={{0,16},{1,17},{2,18},{3,19},{4,20},{5,21},{6,22},{7,23},{8,24},{9,... | collective-permute-start | bytes 49160 | tf_op jit(solution)/shard_map/ppermute | solution.py:57
  93.1 9.8 %collective-permute-start.26 = (bf16[4,3,128,512]{3,2,1,0:T(8,128)(2,1)S(1)}, bf16[4,3,128,512]{3,2,1,0:T(8,128)(2,1)S(1)}, u32[]{:S(2)}, u32[]{:S(2)}) collective-permute-start(bf16[4,3,128,512]{3,2,1,0:T(8,128)(2,1)S(1)} %get-tuple-element.211), channel_id=1, source_target_pairs={{0,1},{1,0},{2,3},{3,2},{4,5},{5,4},{6,7},{7,6},{8,9},{9,8},{10,11... | collective-permute-start | bytes 4718600 | tf_op jit(solution)/shard_map/ppermute | solution.py:57
  93.1 5.1 %collective-permute-start.28 = (bf16[2,4,128,512]{3,2,1,0:T(8,128)(2,1)S(1)}, bf16[2,4,128,512]{3,2,1,0:T(8,128)(2,1)S(1)}, u32[]{:S(2)}, u32[]{:S(2)}) collective-permute-start(bf16[2,4,128,512]{3,2,1,0:T(8,128)(2,1)S(1)} %get-tuple-element.214), channel_id=1, source_target_pairs={{0,1},{1,0},{2,3},{3,2},{4,5},{5,4},{6,7},{7,6},{8,9},{9,8},{10,11... | collective-permute-start | bytes 3145736 | tf_op jit(solution)/shard_map/ppermute | solution.py:57
  101.6 13.8 %collective-permute-start.37 = (bf16[2,2,128,512]{3,2,1,0:T(8,128)(2,1)S(1)}, bf16[2,2,128,512]{3,2,1,0:T(8,128)(2,1)S(1)}, u32[]{:S(2)}, u32[]{:S(2)}) collective-permute-start(bf16[2,2,128,512]{3,2,1,0:T(8,128)(2,1)S(1)} %get-tuple-element.230), channel_id=1, source_target_pairs={{0,8},{1,17},{2,10},{3,19},{4,12},{5,21},{6,14},{7,23},{8,0},{9,25... | collective-permute-start | bytes 1572872 | tf_op jit(solution)/shard_map/ppermute | solution.py:749
  103.3 21.3 %collective-permute-start.30 = (bf16[400,512]{1,0:T(8,128)(2,1)S(1)}, bf16[400,512]{1,0:T(8,128)(2,1)S(1)}, u32[]{:S(2)}, u32[]{:S(2)}) collective-permute-start(bf16[400,512]{1,0:T(8,128)(2,1)S(1)} %get-tuple-element.220), channel_id=1, source_target_pairs={{0,2},{1,3},{2,0},{3,1},{4,6},{5,7},{6,4},{7,5},{8,10},{9,11},{10,... | collective-permute-start | bytes 1228808 | tf_op jit(solution)/shard_map/ppermute | solution.py:57
  104.7 19.8 %collective-permute-start.31 = (bf16[400,512]{1,0:T(8,128)(2,1)S(1)}, bf16[400,512]{1,0:T(8,128)(2,1)S(1)}, u32[]{:S(2)}, u32[]{:S(2)}) collective-permute-start(bf16[400,512]{1,0:T(8,128)(2,1)S(1)} %get-tuple-element.221), channel_id=1, source_target_pairs={{0,4},{1,5},{2,6},{3,7},{4,0},{5,1},{6,2},{7,3},{8,12},{9,13},{10,... | collective-permute-start | bytes 1228808 | tf_op jit(solution)/shard_map/ppermute | solution.py:57
  106.2 18.3 %collective-permute-start.32 = (bf16[400,512]{1,0:T(8,128)(2,1)S(1)}, bf16[400,512]{1,0:T(8,128)(2,1)S(1)}, u32[]{:S(2)}, u32[]{:S(2)}) collective-permute-start(bf16[400,512]{1,0:T(8,128)(2,1)S(1)} %get-tuple-element.222), channel_id=1, source_target_pairs={{0,6},{1,7},{2,4},{3,5},{4,2},{5,3},{6,0},{7,1},{8,14},{9,15},{10,... | collective-permute-start | bytes 1228808 | tf_op jit(solution)/shard_map/ppermute | solution.py:57
  115.5 14.5 %collective-permute-start.38 = (bf16[2,128,512]{2,1,0:T(8,128)(2,1)S(1)}, bf16[2,128,512]{2,1,0:T(8,128)(2,1)S(1)}, u32[]{:S(2)}, u32[]{:S(2)}) collective-permute-start(bf16[2,128,512]{2,1,0:T(8,128)(2,1)S(1)} %get-tuple-element.232), channel_id=1, source_target_pairs={{0,16},{1,9},{2,18},{3,11},{4,20},{5,13},{6,22},{7,15},{8,24},{9,1... | collective-permute-start | bytes 786440 | tf_op jit(solution)/shard_map/ppermute | solution.py:749
  117.2 7.3 %collective-permute-start.33 = (bf16[128,512]{1,0:T(8,128)(2,1)S(1)}, bf16[128,512]{1,0:T(8,128)(2,1)S(1)}, u32[]{:S(2)}, u32[]{:S(2)}) collective-permute-start(bf16[128,512]{1,0:T(8,128)(2,1)S(1)} %get-tuple-element.223), channel_id=1, source_target_pairs={{0,4},{1,3},{2,6},{3,1},{4,0},{5,7},{6,2},{7,5},{8,12},{9,11},{10,... | collective-permute-start | bytes 393224 | tf_op jit(solution)/shard_map/ppermute | solution.py:739
  125.6 10.5 %collective-permute-start.34 = (bf16[144,512]{1,0:T(8,128)(2,1)S(1)}, bf16[144,512]{1,0:T(8,128)(2,1)S(1)}, u32[]{:S(2)}, u32[]{:S(2)}) collective-permute-start(bf16[144,512]{1,0:T(8,128)(2,1)S(1)} %get-tuple-element.226), channel_id=1, source_target_pairs={{0,8},{1,9},{2,10},{3,11},{4,12},{5,13},{6,14},{7,15},{8,0},{9,1},... | collective-permute-start | bytes 442376 | tf_op jit(solution)/shard_map/ppermute | solution.py:57
  126.5 13.9 %collective-permute-start.35 = (bf16[144,512]{1,0:T(8,128)(2,1)S(1)}, bf16[144,512]{1,0:T(8,128)(2,1)S(1)}, u32[]{:S(2)}, u32[]{:S(2)}) collective-permute-start(bf16[144,512]{1,0:T(8,128)(2,1)S(1)} %get-tuple-element.227), channel_id=1, source_target_pairs={{0,16},{1,17},{2,18},{3,19},{4,20},{5,21},{6,22},{7,23},{8,24},{9,... | collective-permute-start | bytes 442376 | tf_op jit(solution)/shard_map/ppermute | solution.py:57
  128.4 12.0 %collective-permute-start.36 = (bf16[144,512]{1,0:T(8,128)(2,1)S(1)}, bf16[144,512]{1,0:T(8,128)(2,1)S(1)}, u32[]{:S(2)}, u32[]{:S(2)}) collective-permute-start(bf16[144,512]{1,0:T(8,128)(2,1)S(1)} %get-tuple-element.228), channel_id=1, source_target_pairs={{0,24},{1,25},{2,26},{3,27},{4,28},{5,29},{6,30},{7,31},{8,16},{9,... | collective-permute-start | bytes 442376 | tf_op jit(solution)/shard_map/ppermute | solution.py:57
  130.1 5.0 %collective-permute-start.39 = (bf16[128,512]{1,0:T(8,128)(2,1)S(1)}, bf16[128,512]{1,0:T(8,128)(2,1)S(1)}, u32[]{:S(2)}, u32[]{:S(2)}) collective-permute-start(bf16[128,512]{1,0:T(8,128)(2,1)S(1)} %get-tuple-element.234), channel_id=1, source_target_pairs={{0,4},{1,3},{2,6},{3,1},{4,0},{5,7},{6,2},{7,5},{8,12},{9,11},{10,... | collective-permute-start | bytes 393224 | tf_op jit(solution)/shard_map/ppermute | solution.py:739
  142.9 4.5 %collective-permute-start.43 = (f32[8,128]{1,0:T(8,128)S(1)}, f32[8,128]{1,0:T(8,128)S(1)}, u32[]{:S(2)}, u32[]{:S(2)}) collective-permute-start(f32[8,128]{1,0:T(8,128)S(1)} %add.38), channel_id=1, source_target_pairs={{0,6},{1,7},{2,4},{3,5},{4,2},{5,3},{6,0},{7,1},{8,14},{9,15},{10,... | collective-permute-start | bytes 12296 | tf_op jit(solution)/shard_map/ppermute | solution.py:57
  149.3 6.0 %collective-permute-start.46 = (f32[8,128]{1,0:T(8,128)S(1)}, f32[8,128]{1,0:T(8,128)S(1)}, u32[]{:S(2)}, u32[]{:S(2)}) collective-permute-start(f32[8,128]{1,0:T(8,128)S(1)} %add_add_fusion.1.squares_ref), channel_id=1, source_target_pairs={{0,24},{1,25},{2,26},{3,27},{4,28},{5,29},{6,30},{7,31},{8,16},{9,... | collective-permute-start | bytes 12296 | tf_op jit(solution)/shard_map/ppermute | solution.py:57
  151.1 4.5 %collective-permute-start.45 = (f32[8,128]{1,0:T(8,128)S(1)}, f32[8,128]{1,0:T(8,128)S(1)}, u32[]{:S(2)}, u32[]{:S(2)}) collective-permute-start(f32[8,128]{1,0:T(8,128)S(1)} %add_add_fusion.1.squares_ref), channel_id=1, source_target_pairs={{0,16},{1,17},{2,18},{3,19},{4,20},{5,21},{6,22},{7,23},{8,24},{9,... | collective-permute-start | bytes 12296 | tf_op jit(solution)/shard_map/ppermute | solution.py:57
  (27 other events, 245.6 us)
where the time goes:
time: 159 us; the launch traced here: 158 us
  waiting for transfers between devices  58.8 us (37%)
  starting transfers between devices  54.9 us (35%)
  Pallas kernels  41.4 us (26%)
  other arithmetic  1.95 us (1%)
    pallas_call x33, Pallas kernels, call(): pl.pallas_call(kernel, in_specs=in_specs, out_specs=jax.tree.map(lambda _...  41.4 us
    ppermute x36, starting transfers between devices, exchange(): return lax.ppermute(value, AXES, pairs)  34.4 us
    ppermute x36, waiting for transfers between devices, exchange(): return lax.ppermute(value, AXES, pairs)  26.9 us
    ppermute x6, waiting for transfers between devices, exchange_z_lane(): return lax.ppermute(value, AXES, pairs)  19.7 us
    ppermute x6, starting transfers between devices, exchange_z_lane(): return lax.ppermute(value, AXES, pairs)  12.9 us
    ppermute x5, waiting for transfers between devices, exchange_lane(): return lax.ppermute(value, AXES, pairs)  12.3 us
    ppermute x5, starting transfers between devices, exchange_lane(): return lax.ppermute(value, AXES, pairs)  7.67 us
  transfers between devices with their start and end apart: 47, of which 26 were waited for; matrix products, arithmetic and copies ran while one was open for 1% of the time, Pallas kernels for 18%

commit v1 on v0

--- a/solution.py
+++ b/solution.py
@@ -1026,9 +1026,8 @@
             gate_pair_kernel, "gate_pair_sum", [near(GATES * ROWS + TAIL, D, dtype=bf16)] * PLANES,
             gate_gown, exchange(gate_gpar, 0, 1), small_terms, small_got, order=[out_keep],
         )
-        gate_round = [gate_parts[0]] + [
-            exchange(part, *bits) for part, bits in zip(gate_parts[1:], PLANE_BITS[1:], strict=True)
-        ]
+        over_both, over_x, over_y = (exchange(gate_parts[k], *PLANE_BITS[k]) for k in (3, 2, 1))
+        gate_round = [gate_parts[0], over_y, over_x, over_both]
         d_x, output, x_done = token_outputs(gate_parts[0])
         out_got = exchange_lane(out_send, False)
         two = near(2, ROWS, D, dtype=bf16)

time: 159 us -> 159 us (level)
  no operation moved by 1% of the time
where the time goes in v1:
time: 159 us; the launch traced here: 158 us
  waiting for transfers between devices  58.8 us (37%)
  starting transfers between devices  54.9 us (35%)
  Pallas kernels  41.4 us (26%)
  other arithmetic  1.95 us (1%)
    pallas_call x33, Pallas kernels, call(): pl.pallas_call(kernel, in_specs=in_specs, out_specs=jax.tree.map(lambda _...  41.4 us
    ppermute x36, starting transfers between devices, exchange(): return lax.ppermute(value, AXES, pairs)  34.4 us
    ppermute x36, waiting for transfers between devices, exchange(): return lax.ppermute(value, AXES, pairs)  26.9 us
    ppermute x6, waiting for transfers between devices, exchange_z_lane(): return lax.ppermute(value, AXES, pairs)  19.7 us
    ppermute x6, starting transfers between devices, exchange_z_lane(): return lax.ppermute(value, AXES, pairs)  12.9 us
    ppermute x5, waiting for transfers between devices, exchange_lane(): return lax.ppermute(value, AXES, pairs)  12.3 us
    ppermute x5, starting transfers between devices, exchange_lane(): return lax.ppermute(value, AXES, pairs)  7.67 us
  transfers between devices with their start and end apart: 47, of which 26 were waited for; matrix products, arithmetic and copies ran while one was open for 1% of the time, Pallas kernels for 18%

profile of v1, /device:TPU:0, one launch (start us, length us, event | category | flops | bytes accessed | tf_op | source)
XLA Modules:
  0.0 158.4 jit_solution(9314119013576163387)
XLA Ops:
  3.5 2.8 %collective-permute-start.1 = (bf16[144,512]{1,0:T(8,128)(2,1)S(1)}, bf16[144,512]{1,0:T(8,128)(2,1)S(1)}, u32[]{:S(2)}, u32[]{:S(2)}) collective-permute-start(bf16[144,512]{1,0:T(8,128)(2,1)S(1)} %mixer_pack.1.first_ref), channel_id=1, source_target_pairs={{0,8},{1,17},{2,10},{3,19},{4,12},{5,21},{6,14},{7,23},{8,0},{9,25... | collective-permute-start | bytes 442376 | tf_op jit(solution)/shard_map/ppermute | solution.py:749
  8.8 1.8 %collective-permute-done.1.second_ref = bf16[144,512]{1,0:T(8,128)(2,1)S(1)} collective-permute-done((bf16[144,512]{1,0:T(8,128)(2,1)S(1)}, bf16[144,512]{1,0:T(8,128)(2,1)S(1)}, u32[]{:S(2)}, u32[]{:S(2)}) %collective-permute-start.1) | collective-permute-done | bytes 147488 | tf_op jit(solution)/shard_map/ppermute | solution.py:749
  10.6 2.8 %collective-permute-start.2 = (bf16[2,144,512]{2,1,0:T(8,128)(2,1)S(1)}, bf16[2,144,512]{2,1,0:T(8,128)(2,1)S(1)}, u32[]{:S(2)}, u32[]{:S(2)}) collective-permute-start(bf16[2,144,512]{2,1,0:T(8,128)(2,1)S(1)} %mixer_pair.1.early_ref), channel_id=1, source_target_pairs={{0,16},{1,9},{2,18},{3,11},{4,20},{5,13},{6,22},{7,15},{8,24},{9,1... | collective-permute-start | bytes 884744 | tf_op jit(solution)/shard_map/ppermute | solution.py:749
  13.4 1.6 %collective-permute-start.4 = (bf16[2,128,512]{2,1,0:T(8,128)(2,1)S(1)}, bf16[2,128,512]{2,1,0:T(8,128)(2,1)S(1)}, u32[]{:S(2)}, u32[]{:S(2)}) collective-permute-start(bf16[2,128,512]{2,1,0:T(8,128)(2,1)S(1)} %mlp_pair.1.first_ref), channel_id=1, source_target_pairs={{0,2},{1,5},{2,0},{3,7},{4,6},{5,1},{6,4},{7,3},{8,10},{9,13},{10,... | collective-permute-start | bytes 786440 | tf_op jit(solution)/shard_map/ppermute | solution.py:739
  15.0 4.9 %collective-permute-done.4.second_ref = bf16[2,128,512]{2,1,0:T(8,128)(2,1)S(1)} collective-permute-done((bf16[2,128,512]{2,1,0:T(8,128)(2,1)S(1)}, bf16[2,128,512]{2,1,0:T(8,128)(2,1)S(1)}, u32[]{:S(2)}, u32[]{:S(2)}) %collective-permute-start.4) | collective-permute-done | bytes 262176 | tf_op jit(solution)/shard_map/ppermute | solution.py:739
  20.7 2.9 %collective-permute-start.8 = (bf16[4,128,512]{2,1,0:T(8,128)(2,1)S(1)}, bf16[4,128,512]{2,1,0:T(8,128)(2,1)S(1)}, u32[]{:S(2)}, u32[]{:S(2)}) collective-permute-start(bf16[4,128,512]{2,1,0:T(8,128)(2,1)S(1)} %mlp_plane.1.refs_0_.first_ref), channel_id=1, source_target_pairs={{0,8},{1,17},{2,10},{3,19},{4,12},{5,21},{6,14},{7,23},{8,0},{9,25... | collective-permute-start | bytes 1572872 | tf_op jit(solution)/shard_map/ppermute | solution.py:749
  23.5 2.4 %collective-permute-start.7 = (bf16[528,512]{1,0:T(8,128)(2,1)S(1)}, bf16[528,512]{1,0:T(8,128)(2,1)S(1)}, u32[]{:S(2)}, u32[]{:S(2)}) collective-permute-start(bf16[528,512]{1,0:T(8,128)(2,1)S(1)} %mixer_slab.1.refs_3_.refs_0_), channel_id=1, source_target_pairs={{0,6},{1,7},{2,4},{3,5},{4,2},{5,3},{6,0},{7,1},{8,14},{9,15},{10,... | collective-permute-start | bytes 1622024 | tf_op jit(solution)/shard_map/ppermute | solution.py:57
  27.0 9.2 %collective-permute-done.8.second_ref = bf16[4,128,512]{2,1,0:T(8,128)(2,1)S(1)} collective-permute-done((bf16[4,128,512]{2,1,0:T(8,128)(2,1)S(1)}, bf16[4,128,512]{2,1,0:T(8,128)(2,1)S(1)}, u32[]{:S(2)}, u32[]{:S(2)}) %collective-permute-start.8) | collective-permute-done | bytes 524320 | tf_op jit(solution)/shard_map/ppermute | solution.py:749
  39.7 9.8 %collective-permute-done.6.refs_5_.refs_2_ = bf16[528,512]{1,0:T(8,128)(2,1)S(1)} collective-permute-done((bf16[528,512]{1,0:T(8,128)(2,1)S(1)}, bf16[528,512]{1,0:T(8,128)(2,1)S(1)}, u32[]{:S(2)}, u32[]{:S(2)}) %collective-permute-start.6) | collective-permute-done | bytes 540704 | tf_op jit(solution)/shard_map/ppermute | solution.py:57
  50.0 2.5 %scan_own.1 = (bf16[512,512]{1,0:T(8,128)(2,1)S(1)}, f32[1,512]{1,0:T(1,128)S(1)}, f32[1,512]{1,0:T(1,128)S(1)}, f32[1,512]{1,0:T(1,128)S(1)}, f32[1,512]{1,0:T(...) custom-call(s32[8]{0:T(128)S(1)} %stack.35.ids_ref.refs_0_, ...), custom_call_target="tpu_custom_call" | custom-call | tf_op jit(solution)/shard_map/scan_own/pallas_call | solution.py:721
  53.0 1.7 %scan_other.1 = (bf16[3,512,512]{2,1,0:T(8,128)(2,1)S(1)}, f32[2,512,512]{2,1,0:T(8,128)S(1)}, f32[4,1024]{1,0:T(4,128)S(1)}, f32[16,512]{1,0:T(8,128)S(1)}, f32[16,512]{1,0:T(8,128)S(1)}) custom-call(bf16[512,512]{1,0:T(8,128)(2,1)S(1)} %get-tuple-element.150.refs_0_.normed_ref.refs_12_, f32[512,1]{1,0:T(8,128)S(1)} %get-tuple-element.142.refs_2_.refs_1_.refs_11_, ...), custom_call_target="tpu_custom_call" | custom-call | tf_op jit(solution)/shard_map/scan_other/pallas_call | solution.py:721
  56.2 2.1 %terms_own.1 = (f32[512,512]{1,0:T(8,128)S(1)}, f32[512,512]{1,0:T(8,128)S(1)}, f32[512,512]{1,0:T(8,128)S(1)}, f32[512,512]{1,0:T(8,128)S(1)}) custom-call(bf16[512,512]{1,0:T(8,128)(2,1)S(1)} %get-tuple-element.150.refs_0_.normed_ref.refs_12_, f32[1,512]{1,0:T(1,128)S(1)} %get-tuple-element.155.fb_ref, f32[1,512]{1,0:T(1,128)S(1)} %get-tuple-element.156.ib_ref, ...), custom_call_target="tpu_custom_call" | custom-call | tf_op jit(solution)/shard_map/terms_own/pallas_call | solution.py:721
  59.4 1.7 %collective-permute-start.15 = (f32[4,1024]{1,0:T(4,128)S(1)}, f32[4,1024]{1,0:T(4,128)S(1)}, u32[]{:S(2)}, u32[]{:S(2)}) collective-permute-start(f32[4,1024]{1,0:T(4,128)S(1)} %get-tuple-element.160.refs_0_), channel_id=1, source_target_pairs={{0,16},{1,17},{2,18},{3,19},{4,20},{5,21},{6,22},{7,23},{8,24},{9,... | collective-permute-start | bytes 49160 | tf_op jit(solution)/shard_map/ppermute | solution.py:57
  61.0 2.5 %collective-permute-start.14 = (f32[4,1024]{1,0:T(4,128)S(1)}, f32[4,1024]{1,0:T(4,128)S(1)}, u32[]{:S(2)}, u32[]{:S(2)}) collective-permute-start(f32[4,1024]{1,0:T(4,128)S(1)} %get-tuple-element.160.refs_0_), channel_id=1, source_target_pairs={{0,8},{1,9},{2,10},{3,11},{4,12},{5,13},{6,14},{7,15},{8,0},{9,1},... | collective-permute-start | bytes 49160 | tf_op jit(solution)/shard_map/ppermute | solution.py:57
  63.5 2.3 %terms_other.1 = (f32[512,512]{1,0:T(8,128)S(1)}, f32[512,512]{1,0:T(8,128)S(1)}, f32[512,512]{1,0:T(8,128)S(1)}, f32[512,512]{1,0:T(8,128)S(1)}) custom-call(bf16[512,512]{1,0:T(8,128)(2,1)S(1)} %get-tuple-element.150.refs_0_.normed_ref.refs_12_, f32[1,512]{1,0:T(1,128)S(1)} %get-tuple-element.151.refs_2_.fb_ref, ...), custom_call_target="tpu_custom_call" | custom-call | tf_op jit(solution)/shard_map/terms_other/pallas_call | solution.py:721
  69.3 7.2 %mlp.1 = (f32[512,512]{1,0:T(8,128)S(1)}, f32[1,512]{1,0:T(1,128)S(1)}, bf16[4,4,128,512]{3,2,1,0:T(8,128)(2,1)S(1)}, bf16[2,4,128,512]{3,2,1,0:T(8,128)(2,1)S(1...) custom-call(s32[8]{0:T(128)S(1)} %stack.35.ids_ref.refs_0_, ...), custom_call_target="tpu_custom_call" | custom-call | tf_op jit(solution)/shard_map/mlp/pallas_call | solution.py:721
  84.4 1.6 %collective-permute-start.25 = (f32[4,1024]{1,0:T(4,128)S(1)}, f32[4,1024]{1,0:T(4,128)S(1)}, u32[]{:S(2)}, u32[]{:S(2)}) collective-permute-start(f32[4,1024]{1,0:T(4,128)S(1)} %get-tuple-element.184.refs_0_), channel_id=1, source_target_pairs={{0,24},{1,25},{2,26},{3,27},{4,28},{5,29},{6,30},{7,31},{8,16},{9,... | collective-permute-start | bytes 49160 | tf_op jit(solution)/shard_map/ppermute | solution.py:57
  87.1 1.7 %collective-permute-start.23 = (f32[4,1024]{1,0:T(4,128)S(1)}, f32[4,1024]{1,0:T(4,128)S(1)}, u32[]{:S(2)}, u32[]{:S(2)}) collective-permute-start(f32[4,1024]{1,0:T(4,128)S(1)} %get-tuple-element.184.refs_0_), channel_id=1, source_target_pairs={{0,8},{1,9},{2,10},{3,11},{4,12},{5,13},{6,14},{7,15},{8,0},{9,1},... | collective-permute-start | bytes 49160 | tf_op jit(solution)/shard_map/ppermute | solution.py:57
  91.4 1.7 %gates_other.1 = (bf16[4,3,128,512]{3,2,1,0:T(8,128)(2,1)S(1)}, bf16[512,512]{1,0:T(8,128)(2,1)S(1)}, bf16[512,512]{1,0:T(8,128)(2,1)S(1)}, bf16[512,512]{1,0:T(...) custom-call(f32[2,1024]{1,0:T(2,128)S(1)} %relay_far.3.refs_0_, f32[2,1024]{1,0:T(2,128)S(1)} %relay_far.2.inc_ref.refs_1_, ...), custom_call_target="tpu_custom_call" | custom-call | tf_op jit(solution)/shard_map/gates_other/pallas_call | solution.py:721
  93.6 1.7 %gates_own.1 = (bf16[4,3,128,512]{3,2,1,0:T(8,128)(2,1)S(1)}, bf16[512,512]{1,0:T(8,128)(2,1)S(1)}, bf16[512,512]{1,0:T(8,128)(2,1)S(1)}, bf16[512,512]{1,0:T(8,...) custom-call(f32[2,1024]{1,0:T(2,128)S(1)} %relay_far.3.refs_0_, f32[2,1024]{1,0:T(2,128)S(1)} %relay_far.2.inc_ref.refs_1_, ...), custom_call_target="tpu_custom_call" | custom-call | tf_op jit(solution)/shard_map/gates_own/pallas_call | solution.py:721
  95.3 2.8 %input_terms.1 = (f32[512,512]{1,0:T(8,128)S(1)}, f32[16,512]{1,0:T(8,128)S(1)}) custom-call(s32[8]{0:T(128)S(1)} %stack.35.ids_ref.refs_0_, bf16[2,256,512]{2,1,0:T(8,128)(2,1)S(1)} %copy-done, f32[1,512]{1,0:T(1,128)S(1)} %get-tuple-element.174.dgain_two_ref, f32[1,512]{1,0:T(1,128)S(1)} %get-tuple-element.198.dfb_o.refs_8_, ...), custom_call_target="tpu_custom_call" | custom-call | tf_op jit(solution)/shard_map/input_terms/pallas_call | solution.py:721
  106.8 8.6 %collective-permute-done.37.got_ref = bf16[2,2,128,512]{3,2,1,0:T(8,128)(2,1)S(1)} collective-permute-done((bf16[2,2,128,512]{3,2,1,0:T(8,128)(2,1)S(1)}, bf16[2,2,128,512]{3,2,1,0:T(8,128)(2,1)S(1)}, u32[]{:S(2)}, u32[]{:S(2)}) %collective-permute-start.37) | collective-permute-done | bytes 524320 | tf_op jit(solution)/shard_map/ppermute | solution.py:749
  115.5 1.7 %collective-permute-start.38 = (bf16[2,128,512]{2,1,0:T(8,128)(2,1)S(1)}, bf16[2,128,512]{2,1,0:T(8,128)(2,1)S(1)}, u32[]{:S(2)}, u32[]{:S(2)}) collective-permute-start(bf16[2,128,512]{2,1,0:T(8,128)(2,1)S(1)} %get-tuple-element.232), channel_id=1, source_target_pairs={{0,16},{1,9},{2,18},{3,11},{4,20},{5,13},{6,22},{7,15},{8,24},{9,1... | collective-permute-start | bytes 786440 | tf_op jit(solution)/shard_map/ppermute | solution.py:749
  118.7 3.0 %outputs.1 = (bf16[2,256,512]{2,1,0:T(8,128)(2,1)}, bf16[2,256,512]{2,1,0:T(8,128)(2,1)}, f32[8,128]{1,0:T(8,128)S(1)}) custom-call(bf16[2,256,512]{2,1,0:T(8,128)(2,1)S(1)} %copy-done, f32[1,512]{1,0:T(1,128)S(1)} %get-tuple-element.149.gain_ref, f32[512,512]{1,0:T(8,128)S(1)} %get-tuple-element.173.dresid_ref, ...), custom_call_target="tpu_custom_call" | custom-call | tf_op jit(solution)/shard_map/outputs/pallas_call | solution.py:721
  121.7 2.8 %collective-permute-done.33.out_got = bf16[128,512]{1,0:T(8,128)(2,1)S(1)} collective-permute-done((bf16[128,512]{1,0:T(8,128)(2,1)S(1)}, bf16[128,512]{1,0:T(8,128)(2,1)S(1)}, u32[]{:S(2)}, u32[]{:S(2)}) %collective-permute-start.33) | collective-permute-done | bytes 131104 | tf_op jit(solution)/shard_map/ppermute | solution.py:739
  126.5 2.0 %collective-permute-start.35 = (bf16[144,512]{1,0:T(8,128)(2,1)S(1)}, bf16[144,512]{1,0:T(8,128)(2,1)S(1)}, u32[]{:S(2)}, u32[]{:S(2)}) collective-permute-start(bf16[144,512]{1,0:T(8,128)(2,1)S(1)} %get-tuple-element.227), channel_id=1, source_target_pairs={{0,16},{1,17},{2,18},{3,19},{4,20},{5,21},{6,22},{7,23},{8,24},{9,... | collective-permute-start | bytes 442376 | tf_op jit(solution)/shard_map/ppermute | solution.py:57
  128.4 1.6 %collective-permute-start.36 = (bf16[144,512]{1,0:T(8,128)(2,1)S(1)}, bf16[144,512]{1,0:T(8,128)(2,1)S(1)}, u32[]{:S(2)}, u32[]{:S(2)}) collective-permute-start(bf16[144,512]{1,0:T(8,128)(2,1)S(1)} %get-tuple-element.228), channel_id=1, source_target_pairs={{0,24},{1,25},{2,26},{3,27},{4,28},{5,29},{6,30},{7,31},{8,16},{9,... | collective-permute-start | bytes 442376 | tf_op jit(solution)/shard_map/ppermute | solution.py:57
  131.7 3.5 %collective-permute-done.39.got_ref = bf16[128,512]{1,0:T(8,128)(2,1)S(1)} collective-permute-done((bf16[128,512]{1,0:T(8,128)(2,1)S(1)}, bf16[128,512]{1,0:T(8,128)(2,1)S(1)}, u32[]{:S(2)}, u32[]{:S(2)}) %collective-permute-start.39) | collective-permute-done | bytes 131104 | tf_op jit(solution)/shard_map/ppermute | solution.py:739
  136.1 4.3 %collective-permute-done.35.g2_ref = bf16[144,512]{1,0:T(8,128)(2,1)S(1)} collective-permute-done((bf16[144,512]{1,0:T(8,128)(2,1)S(1)}, bf16[144,512]{1,0:T(8,128)(2,1)S(1)}, u32[]{:S(2)}, u32[]{:S(2)}) %collective-permute-start.35) | collective-permute-done | bytes 147488 | tf_op jit(solution)/shard_map/ppermute | solution.py:57
  142.9 2.3 %collective-permute-start.43 = (f32[8,128]{1,0:T(8,128)S(1)}, f32[8,128]{1,0:T(8,128)S(1)}, u32[]{:S(2)}, u32[]{:S(2)}) collective-permute-start(f32[8,128]{1,0:T(8,128)S(1)} %add.38), channel_id=1, source_target_pairs={{0,6},{1,7},{2,4},{3,5},{4,2},{5,3},{6,0},{7,1},{8,14},{9,15},{10,... | collective-permute-start | bytes 12296 | tf_op jit(solution)/shard_map/ppermute | solution.py:57
  149.3 1.8 %collective-permute-start.46 = (f32[8,128]{1,0:T(8,128)S(1)}, f32[8,128]{1,0:T(8,128)S(1)}, u32[]{:S(2)}, u32[]{:S(2)}) collective-permute-start(f32[8,128]{1,0:T(8,128)S(1)} %add_add_fusion.1.squares_ref), channel_id=1, source_target_pairs={{0,24},{1,25},{2,26},{3,27},{4,28},{5,29},{6,30},{7,31},{8,16},{9,... | collective-permute-start | bytes 12296 | tf_op jit(solution)/shard_map/ppermute | solution.py:57
  151.1 2.3 %collective-permute-start.45 = (f32[8,128]{1,0:T(8,128)S(1)}, f32[8,128]{1,0:T(8,128)S(1)}, u32[]{:S(2)}, u32[]{:S(2)}) collective-permute-start(f32[8,128]{1,0:T(8,128)S(1)} %add_add_fusion.1.squares_ref), channel_id=1, source_target_pairs={{0,16},{1,17},{2,18},{3,19},{4,20},{5,21},{6,22},{7,23},{8,24},{9,... | collective-permute-start | bytes 12296 | tf_op jit(solution)/shard_map/ppermute | solution.py:57
  (125 shorter events, 56.1 us)
Async XLA Ops:
  3.5 7.1 %collective-permute-start.1 = (bf16[144,512]{1,0:T(8,128)(2,1)S(1)}, bf16[144,512]{1,0:T(8,128)(2,1)S(1)}, u32[]{:S(2)}, u32[]{:S(2)}) collective-permute-start(bf16[144,512]{1,0:T(8,128)(2,1)S(1)} %mixer_pack.1.first_ref), channel_id=1, source_target_pairs={{0,8},{1,17},{2,10},{3,19},{4,12},{5,21},{6,14},{7,23},{8,0},{9,25... | collective-permute-start | bytes 442376 | tf_op jit(solution)/shard_map/ppermute | solution.py:749
  7.3 6.1 %collective-permute-start.3 = (bf16[128,512]{1,0:T(8,128)(2,1)S(1)}, bf16[128,512]{1,0:T(8,128)(2,1)S(1)}, u32[]{:S(2)}, u32[]{:S(2)}) collective-permute-start(bf16[128,512]{1,0:T(8,128)(2,1)S(1)} %convert_element_type.7.first_ref), channel_id=1, source_target_pairs={{0,4},{1,3},{2,6},{3,1},{4,0},{5,7},{6,2},{7,5},{8,12},{9,11},{10,... | collective-permute-start | bytes 393224 | tf_op jit(solution)/shard_map/ppermute | solution.py:739
  10.6 9.4 %collective-permute-start.2 = (bf16[2,144,512]{2,1,0:T(8,128)(2,1)S(1)}, bf16[2,144,512]{2,1,0:T(8,128)(2,1)S(1)}, u32[]{:S(2)}, u32[]{:S(2)}) collective-permute-start(bf16[2,144,512]{2,1,0:T(8,128)(2,1)S(1)} %mixer_pair.1.early_ref), channel_id=1, source_target_pairs={{0,16},{1,9},{2,18},{3,11},{4,20},{5,13},{6,22},{7,15},{8,24},{9,1... | collective-permute-start | bytes 884744 | tf_op jit(solution)/shard_map/ppermute | solution.py:749
  13.4 6.4 %collective-permute-start.4 = (bf16[2,128,512]{2,1,0:T(8,128)(2,1)S(1)}, bf16[2,128,512]{2,1,0:T(8,128)(2,1)S(1)}, u32[]{:S(2)}, u32[]{:S(2)}) collective-permute-start(bf16[2,128,512]{2,1,0:T(8,128)(2,1)S(1)} %mlp_pair.1.first_ref), channel_id=1, source_target_pairs={{0,2},{1,5},{2,0},{3,7},{4,6},{5,1},{6,4},{7,3},{8,10},{9,13},{10,... | collective-permute-start | bytes 786440 | tf_op jit(solution)/shard_map/ppermute | solution.py:739
  20.7 15.6 %collective-permute-start.8 = (bf16[4,128,512]{2,1,0:T(8,128)(2,1)S(1)}, bf16[4,128,512]{2,1,0:T(8,128)(2,1)S(1)}, u32[]{:S(2)}, u32[]{:S(2)}) collective-permute-start(bf16[4,128,512]{2,1,0:T(8,128)(2,1)S(1)} %mlp_plane.1.refs_0_.first_ref), channel_id=1, source_target_pairs={{0,8},{1,17},{2,10},{3,19},{4,12},{5,21},{6,14},{7,23},{8,0},{9,25... | collective-permute-start | bytes 1572872 | tf_op jit(solution)/shard_map/ppermute | solution.py:749
  23.5 16.2 %collective-permute-start.7 = (bf16[528,512]{1,0:T(8,128)(2,1)S(1)}, bf16[528,512]{1,0:T(8,128)(2,1)S(1)}, u32[]{:S(2)}, u32[]{:S(2)}) collective-permute-start(bf16[528,512]{1,0:T(8,128)(2,1)S(1)} %mixer_slab.1.refs_3_.refs_0_), channel_id=1, source_target_pairs={{0,6},{1,7},{2,4},{3,5},{4,2},{5,3},{6,0},{7,1},{8,14},{9,15},{10,... | collective-permute-start | bytes 1622024 | tf_op jit(solution)/shard_map/ppermute | solution.py:57
  26.0 23.5 %collective-permute-start.6 = (bf16[528,512]{1,0:T(8,128)(2,1)S(1)}, bf16[528,512]{1,0:T(8,128)(2,1)S(1)}, u32[]{:S(2)}, u32[]{:S(2)}) collective-permute-start(bf16[528,512]{1,0:T(8,128)(2,1)S(1)} %mixer_slab.1.refs_3_.refs_0_), channel_id=1, source_target_pairs={{0,4},{1,5},{2,6},{3,7},{4,0},{5,1},{6,2},{7,3},{8,12},{9,13},{10,... | collective-permute-start | bytes 1622024 | tf_op jit(solution)/shard_map/ppermute | solution.py:57
  26.5 23.0 %collective-permute-start.5 = (bf16[528,512]{1,0:T(8,128)(2,1)S(1)}, bf16[528,512]{1,0:T(8,128)(2,1)S(1)}, u32[]{:S(2)}, u32[]{:S(2)}) collective-permute-start(bf16[528,512]{1,0:T(8,128)(2,1)S(1)} %mixer_slab.1.refs_3_.refs_0_), channel_id=1, source_target_pairs={{0,2},{1,3},{2,0},{3,1},{4,6},{5,7},{6,4},{7,5},{8,10},{9,11},{10,... | collective-permute-start | bytes 1622024 | tf_op jit(solution)/shard_map/ppermute | solution.py:57
  36.3 30.1 %collective-permute-start.17 = (bf16[2,4,128,512]{3,2,1,0:T(8,128)(2,1)S(1)}, bf16[2,4,128,512]{3,2,1,0:T(8,128)(2,1)S(1)}, u32[]{:S(2)}, u32[]{:S(2)}) collective-permute-start(bf16[2,4,128,512]{3,2,1,0:T(8,128)(2,1)S(1)} %mlp_early.1.refs_0_), channel_id=1, source_target_pairs={{0,16},{1,9},{2,18},{3,11},{4,20},{5,13},{6,22},{7,15},{8,24},{9,1... | collective-permute-start | bytes 3145736 | tf_op jit(solution)/shard_map/ppermute | solution.py:749
  39.1 13.4 %collective-permute-start.9 = (bf16[528,512]{1,0:T(8,128)(2,1)S(1)}, bf16[528,512]{1,0:T(8,128)(2,1)S(1)}, u32[]{:S(2)}, u32[]{:S(2)}) collective-permute-start(bf16[528,512]{1,0:T(8,128)(2,1)S(1)} %mixer_slab.1.refs_3_.refs_0_), channel_id=1, source_target_pairs={{0,1},{1,0},{2,3},{3,2},{4,5},{5,4},{6,7},{7,6},{8,9},{9,8},{10,11... | collective-permute-start | bytes 1622024 | tf_op jit(solution)/shard_map/ppermute | solution.py:57
  59.0 6.8 %collective-permute-start.16 = (f32[4,1024]{1,0:T(4,128)S(1)}, f32[4,1024]{1,0:T(4,128)S(1)}, u32[]{:S(2)}, u32[]{:S(2)}) collective-permute-start(f32[4,1024]{1,0:T(4,128)S(1)} %get-tuple-element.160.refs_0_), channel_id=1, source_target_pairs={{0,24},{1,25},{2,26},{3,27},{4,28},{5,29},{6,30},{7,31},{8,16},{9,... | collective-permute-start | bytes 49160 | tf_op jit(solution)/shard_map/ppermute | solution.py:57
  59.4 6.5 %collective-permute-start.15 = (f32[4,1024]{1,0:T(4,128)S(1)}, f32[4,1024]{1,0:T(4,128)S(1)}, u32[]{:S(2)}, u32[]{:S(2)}) collective-permute-start(f32[4,1024]{1,0:T(4,128)S(1)} %get-tuple-element.160.refs_0_), channel_id=1, source_target_pairs={{0,16},{1,17},{2,18},{3,19},{4,20},{5,21},{6,22},{7,23},{8,24},{9,... | collective-permute-start | bytes 49160 | tf_op jit(solution)/shard_map/ppermute | solution.py:57
  61.0 4.8 %collective-permute-start.14 = (f32[4,1024]{1,0:T(4,128)S(1)}, f32[4,1024]{1,0:T(4,128)S(1)}, u32[]{:S(2)}, u32[]{:S(2)}) collective-permute-start(f32[4,1024]{1,0:T(4,128)S(1)} %get-tuple-element.160.refs_0_), channel_id=1, source_target_pairs={{0,8},{1,9},{2,10},{3,11},{4,12},{5,13},{6,14},{7,15},{8,0},{9,1},... | collective-permute-start | bytes 49160 | tf_op jit(solution)/shard_map/ppermute | solution.py:57
  63.5 4.5 %collective-permute-start.18 = (bf16[2,4,128,512]{3,2,1,0:T(8,128)(2,1)S(1)}, bf16[2,4,128,512]{3,2,1,0:T(8,128)(2,1)S(1)}, u32[]{:S(2)}, u32[]{:S(2)}) collective-permute-start(bf16[2,4,128,512]{3,2,1,0:T(8,128)(2,1)S(1)} %mlp_early.1.refs_0_), channel_id=1, source_target_pairs={{0,1},{1,0},{2,3},{3,2},{4,5},{5,4},{6,7},{7,6},{8,9},{9,8},{10,11... | collective-permute-start | bytes 3145736 | tf_op jit(solution)/shard_map/ppermute | solution.py:57
  82.9 17.7 %collective-permute-start.29 = (bf16[2,5,128,512]{3,2,1,0:T(8,128)(2,1)S(1)}, bf16[2,5,128,512]{3,2,1,0:T(8,128)(2,1)S(1)}, u32[]{:S(2)}, u32[]{:S(2)}) collective-permute-start(bf16[2,5,128,512]{3,2,1,0:T(8,128)(2,1)S(1)} %mlp_pair_sum.1.refs_0_), channel_id=1, source_target_pairs={{0,2},{1,5},{2,0},{3,7},{4,6},{5,1},{6,4},{7,3},{8,10},{9,13},{10,... | collective-permute-start | bytes 3932168 | tf_op jit(solution)/shard_map/ppermute | solution.py:739
  84.4 5.5 %collective-permute-start.25 = (f32[4,1024]{1,0:T(4,128)S(1)}, f32[4,1024]{1,0:T(4,128)S(1)}, u32[]{:S(2)}, u32[]{:S(2)}) collective-permute-start(f32[4,1024]{1,0:T(4,128)S(1)} %get-tuple-element.184.refs_0_), channel_id=1, source_target_pairs={{0,24},{1,25},{2,26},{3,27},{4,28},{5,29},{6,30},{7,31},{8,16},{9,... | collective-permute-start | bytes 49160 | tf_op jit(solution)/shard_map/ppermute | solution.py:57
  86.0 4.6 %collective-permute-start.24 = (f32[4,1024]{1,0:T(4,128)S(1)}, f32[4,1024]{1,0:T(4,128)S(1)}, u32[]{:S(2)}, u32[]{:S(2)}) collective-permute-start(f32[4,1024]{1,0:T(4,128)S(1)} %get-tuple-element.184.refs_0_), channel_id=1, source_target_pairs={{0,16},{1,17},{2,18},{3,19},{4,20},{5,21},{6,22},{7,23},{8,24},{9,... | collective-permute-start | bytes 49160 | tf_op jit(solution)/shard_map/ppermute | solution.py:57
  93.1 9.8 %collective-permute-start.26 = (bf16[4,3,128,512]{3,2,1,0:T(8,128)(2,1)S(1)}, bf16[4,3,128,512]{3,2,1,0:T(8,128)(2,1)S(1)}, u32[]{:S(2)}, u32[]{:S(2)}) collective-permute-start(bf16[4,3,128,512]{3,2,1,0:T(8,128)(2,1)S(1)} %get-tuple-element.211), channel_id=1, source_target_pairs={{0,1},{1,0},{2,3},{3,2},{4,5},{5,4},{6,7},{7,6},{8,9},{9,8},{10,11... | collective-permute-start | bytes 4718600 | tf_op jit(solution)/shard_map/ppermute | solution.py:57
  93.1 5.1 %collective-permute-start.28 = (bf16[2,4,128,512]{3,2,1,0:T(8,128)(2,1)S(1)}, bf16[2,4,128,512]{3,2,1,0:T(8,128)(2,1)S(1)}, u32[]{:S(2)}, u32[]{:S(2)}) collective-permute-start(bf16[2,4,128,512]{3,2,1,0:T(8,128)(2,1)S(1)} %get-tuple-element.214), channel_id=1, source_target_pairs={{0,1},{1,0},{2,3},{3,2},{4,5},{5,4},{6,7},{7,6},{8,9},{9,8},{10,11... | collective-permute-start | bytes 3145736 | tf_op jit(solution)/shard_map/ppermute | solution.py:57
  101.6 13.8 %collective-permute-start.37 = (bf16[2,2,128,512]{3,2,1,0:T(8,128)(2,1)S(1)}, bf16[2,2,128,512]{3,2,1,0:T(8,128)(2,1)S(1)}, u32[]{:S(2)}, u32[]{:S(2)}) collective-permute-start(bf16[2,2,128,512]{3,2,1,0:T(8,128)(2,1)S(1)} %get-tuple-element.230), channel_id=1, source_target_pairs={{0,8},{1,17},{2,10},{3,19},{4,12},{5,21},{6,14},{7,23},{8,0},{9,25... | collective-permute-start | bytes 1572872 | tf_op jit(solution)/shard_map/ppermute | solution.py:749
  103.3 21.3 %collective-permute-start.30 = (bf16[400,512]{1,0:T(8,128)(2,1)S(1)}, bf16[400,512]{1,0:T(8,128)(2,1)S(1)}, u32[]{:S(2)}, u32[]{:S(2)}) collective-permute-start(bf16[400,512]{1,0:T(8,128)(2,1)S(1)} %get-tuple-element.220), channel_id=1, source_target_pairs={{0,2},{1,3},{2,0},{3,1},{4,6},{5,7},{6,4},{7,5},{8,10},{9,11},{10,... | collective-permute-start | bytes 1228808 | tf_op jit(solution)/shard_map/ppermute | solution.py:57
  104.7 19.8 %collective-permute-start.31 = (bf16[400,512]{1,0:T(8,128)(2,1)S(1)}, bf16[400,512]{1,0:T(8,128)(2,1)S(1)}, u32[]{:S(2)}, u32[]{:S(2)}) collective-permute-start(bf16[400,512]{1,0:T(8,128)(2,1)S(1)} %get-tuple-element.221), channel_id=1, source_target_pairs={{0,4},{1,5},{2,6},{3,7},{4,0},{5,1},{6,2},{7,3},{8,12},{9,13},{10,... | collective-permute-start | bytes 1228808 | tf_op jit(solution)/shard_map/ppermute | solution.py:57
  106.2 18.3 %collective-permute-start.32 = (bf16[400,512]{1,0:T(8,128)(2,1)S(1)}, bf16[400,512]{1,0:T(8,128)(2,1)S(1)}, u32[]{:S(2)}, u32[]{:S(2)}) collective-permute-start(bf16[400,512]{1,0:T(8,128)(2,1)S(1)} %get-tuple-element.222), channel_id=1, source_target_pairs={{0,6},{1,7},{2,4},{3,5},{4,2},{5,3},{6,0},{7,1},{8,14},{9,15},{10,... | collective-permute-start | bytes 1228808 | tf_op jit(solution)/shard_map/ppermute | solution.py:57
  115.5 14.5 %collective-permute-start.38 = (bf16[2,128,512]{2,1,0:T(8,128)(2,1)S(1)}, bf16[2,128,512]{2,1,0:T(8,128)(2,1)S(1)}, u32[]{:S(2)}, u32[]{:S(2)}) collective-permute-start(bf16[2,128,512]{2,1,0:T(8,128)(2,1)S(1)} %get-tuple-element.232), channel_id=1, source_target_pairs={{0,16},{1,9},{2,18},{3,11},{4,20},{5,13},{6,22},{7,15},{8,24},{9,1... | collective-permute-start | bytes 786440 | tf_op jit(solution)/shard_map/ppermute | solution.py:749
  117.2 7.3 %collective-permute-start.33 = (bf16[128,512]{1,0:T(8,128)(2,1)S(1)}, bf16[128,512]{1,0:T(8,128)(2,1)S(1)}, u32[]{:S(2)}, u32[]{:S(2)}) collective-permute-start(bf16[128,512]{1,0:T(8,128)(2,1)S(1)} %get-tuple-element.223), channel_id=1, source_target_pairs={{0,4},{1,3},{2,6},{3,1},{4,0},{5,7},{6,2},{7,5},{8,12},{9,11},{10,... | collective-permute-start | bytes 393224 | tf_op jit(solution)/shard_map/ppermute | solution.py:739
  125.6 10.5 %collective-permute-start.34 = (bf16[144,512]{1,0:T(8,128)(2,1)S(1)}, bf16[144,512]{1,0:T(8,128)(2,1)S(1)}, u32[]{:S(2)}, u32[]{:S(2)}) collective-permute-start(bf16[144,512]{1,0:T(8,128)(2,1)S(1)} %get-tuple-element.226), channel_id=1, source_target_pairs={{0,8},{1,9},{2,10},{3,11},{4,12},{5,13},{6,14},{7,15},{8,0},{9,1},... | collective-permute-start | bytes 442376 | tf_op jit(solution)/shard_map/ppermute | solution.py:57
  126.5 13.9 %collective-permute-start.35 = (bf16[144,512]{1,0:T(8,128)(2,1)S(1)}, bf16[144,512]{1,0:T(8,128)(2,1)S(1)}, u32[]{:S(2)}, u32[]{:S(2)}) collective-permute-start(bf16[144,512]{1,0:T(8,128)(2,1)S(1)} %get-tuple-element.227), channel_id=1, source_target_pairs={{0,16},{1,17},{2,18},{3,19},{4,20},{5,21},{6,22},{7,23},{8,24},{9,... | collective-permute-start | bytes 442376 | tf_op jit(solution)/shard_map/ppermute | solution.py:57
  128.4 12.0 %collective-permute-start.36 = (bf16[144,512]{1,0:T(8,128)(2,1)S(1)}, bf16[144,512]{1,0:T(8,128)(2,1)S(1)}, u32[]{:S(2)}, u32[]{:S(2)}) collective-permute-start(bf16[144,512]{1,0:T(8,128)(2,1)S(1)} %get-tuple-element.228), channel_id=1, source_target_pairs={{0,24},{1,25},{2,26},{3,27},{4,28},{5,29},{6,30},{7,31},{8,16},{9,... | collective-permute-start | bytes 442376 | tf_op jit(solution)/shard_map/ppermute | solution.py:57
  130.1 5.0 %collective-permute-start.39 = (bf16[128,512]{1,0:T(8,128)(2,1)S(1)}, bf16[128,512]{1,0:T(8,128)(2,1)S(1)}, u32[]{:S(2)}, u32[]{:S(2)}) collective-permute-start(bf16[128,512]{1,0:T(8,128)(2,1)S(1)} %get-tuple-element.234), channel_id=1, source_target_pairs={{0,4},{1,3},{2,6},{3,1},{4,0},{5,7},{6,2},{7,5},{8,12},{9,11},{10,... | collective-permute-start | bytes 393224 | tf_op jit(solution)/shard_map/ppermute | solution.py:739
  142.9 4.5 %collective-permute-start.43 = (f32[8,128]{1,0:T(8,128)S(1)}, f32[8,128]{1,0:T(8,128)S(1)}, u32[]{:S(2)}, u32[]{:S(2)}) collective-permute-start(f32[8,128]{1,0:T(8,128)S(1)} %add.38), channel_id=1, source_target_pairs={{0,6},{1,7},{2,4},{3,5},{4,2},{5,3},{6,0},{7,1},{8,14},{9,15},{10,... | collective-permute-start | bytes 12296 | tf_op jit(solution)/shard_map/ppermute | solution.py:57
  149.3 6.0 %collective-permute-start.46 = (f32[8,128]{1,0:T(8,128)S(1)}, f32[8,128]{1,0:T(8,128)S(1)}, u32[]{:S(2)}, u32[]{:S(2)}) collective-permute-start(f32[8,128]{1,0:T(8,128)S(1)} %add_add_fusion.1.squares_ref), channel_id=1, source_target_pairs={{0,24},{1,25},{2,26},{3,27},{4,28},{5,29},{6,30},{7,31},{8,16},{9,... | collective-permute-start | bytes 12296 | tf_op jit(solution)/shard_map/ppermute | solution.py:57
  151.1 4.5 %collective-permute-start.45 = (f32[8,128]{1,0:T(8,128)S(1)}, f32[8,128]{1,0:T(8,128)S(1)}, u32[]{:S(2)}, u32[]{:S(2)}) collective-permute-start(f32[8,128]{1,0:T(8,128)S(1)} %add_add_fusion.1.squares_ref), channel_id=1, source_target_pairs={{0,16},{1,17},{2,18},{3,19},{4,20},{5,21},{6,22},{7,23},{8,24},{9,... | collective-permute-start | bytes 12296 | tf_op jit(solution)/shard_map/ppermute | solution.py:57
  (27 other events, 245.6 us)
